TPU v7x, 768 devices: a whole 4x8x12 slice. The times are simulated.
768 devices in a mesh: space: 64 (over x, y, core), segment: 12 (over z).
Axes of the slice: x: 4, y: 8, z: 12, core: 2. Of those that a mesh axis runs over, the one named last changes fastest.
Arguments:
- incoming: bfloat16 [12, 1024, 64, 128], P('segment', 'space'), may hold values from -6 to 6
- saved: bfloat16 [12, 1024, 64, 128], P('segment', 'space'), may hold values from -6 to 6
- cotangent: bfloat16 [12, 1024, 64, 128], P('segment', 'space'), may hold values from -6 to 6
- occupancy: int32 [12, 1024, 64], P('segment', 'space'), may hold values from 0 to 1, as said below
- neighbours: int32 [12, 1024, 27], P('segment', 'space'), may hold values from -1 to 1023, as said below
- conv_weight: bfloat16 [12, 27, 128, 128], P('segment'), may hold values from -0.15625 to 0.15625
Outputs:
- arrived: bfloat16 [12, 1024, 64, 128], P('segment', 'space')
- returned: bfloat16 [12, 1024, 64, 128], P('segment', 'space')
Inputs may be any that keep to these rules, and one draw needn't show every extreme that they name: `neighbours`: per section: entry o = 9 (ex + 1) + 3 (ey + 1) + (ez + 1) of brick b names the brick at brick offset (ex, ey, ez) from b, or -1 where there is none. A named brick's number differs from b by at most 7. The relation is symmetric: b names c at o exactly when c names b at 26 - o. A present brick names itself at entry 13; a brick slot that is not present has all entries -1, no occupied voxel, and is named by no brick. `occupancy`: voxel u = 16 x + 4 y + z of a brick.
All inputs are finite; a program needn't handle non-finite values.
Results may differ from a plain program's by a relative error of at most 0.0034.
Values may be sent and summed in bfloat16 or wider, within the bound.
No kernel may reach another device: no remote copies, remote signals or barrier semaphores. Data moves between devices by JAX's collectives and lax.ppermute only.
A program may use at most 128 MiB of HBM per device.

v0:
```python
import functools

import jax
import jax.numpy as jnp
from jax import lax
from jax.experimental import pallas as pl
from jax.experimental.pallas import tpu as pltpu
from jax.sharding import PartitionSpec as P

BF16 = jnp.bfloat16
F32 = jnp.float32
STEPS = (-1, 0, 1)
VMEM_LIMIT = 40 * 1024 * 1024


def source_coordinate(step, c):
    return c if step == 0 else (3 if step < 0 else 0)


def padded_coordinate(step, c):
    return c + 1 if step == 0 else (0 if step < 0 else 5)


def offset_index(ex, ey, ez):
    return 9 * (ex + 1) + 3 * (ey + 1) + (ez + 1)


def gather_plan():
    matrices, plan, mixed = [], [], []
    corners = {-1: [], 1: []}
    for ex in STEPS:
        for ey in STEPS:
            for ez in STEPS:
                steps = (ex, ey, ez)
                zeros = [a for a in range(3) if steps[a] == 0]
                if len(zeros) == 3:
                    continue
                o = offset_index(ex, ey, ez)

                def cell(c):
                    source = [source_coordinate(s, v) for s, v in zip(steps, c)]
                    padded = [padded_coordinate(s, v) for s, v in zip(steps, c)]
                    return (o, tuple(padded), tuple(source))

                if not zeros:
                    corners[ey].append(cell((0, 0, 0)))
                    continue
                along = zeros[0] if len(zeros) == 1 else max(a for a in zeros if a != 1)
                index = len(matrices)
                matrices.append((o,) * 4)
                if along == 1:
                    mixed.append(index)
                outer = [a for a in zeros if a != along]
                for first in range(4) if outer else (0,):
                    cells = []
                    for second in range(4):
                        c = [0, 0, 0]
                        c[along] = second
                        if outer:
                            c[outer[0]] = first
                        cells.append(cell(c))
                    plan.append((index, cells))
    for ey in (-1, 1):
        plan.append((len(matrices), corners[ey]))
        matrices.append(tuple(c[0] for c in corners[ey]))
    return matrices, plan, mixed


MATRICES, PLAN, MIXED = gather_plan()
COUNT = len(MATRICES)


def permutation(mask):
    row = lax.broadcasted_iota(jnp.int32, (256, 256), 0)
    column = lax.broadcasted_iota(jnp.int32, (256, 256), 1)
    hit = column == ((row & 15) * 16 + (row >> 4))
    repeated = jnp.concatenate([mask] * 16, axis=0)
    return jnp.where(hit, repeated, 0.0).astype(BF16)


def rows_mask(occ, block):
    u = lax.broadcasted_iota(jnp.int32, (64, 256), 0)
    column = lax.broadcasted_iota(jnp.int32, (64, 256), 1)
    spread = jnp.where(u == 16 * block + (column & 15), 1.0, 0.0).astype(BF16)
    return jnp.dot(occ, spread, preferred_element_type=F32)


def columns_mask(occ):
    b = lax.broadcasted_iota(jnp.int32, (16, 256), 0)
    column = lax.broadcasted_iota(jnp.int32, (16, 256), 1)
    spread = jnp.where(b == (column & 15), 1.0, 0.0).astype(BF16)
    return lax.dot_general(occ, spread, (((0,), (0,)), ((), ())), preferred_element_type=F32)


def voxel_major(ref, block, matrix):
    rows = ref[:, 16 * block : 16 * block + 16, :].reshape(256, 128)
    return jnp.dot(matrix, rows, preferred_element_type=F32).reshape(16, 16, 128)


def fetch(sources, targets, sems):
    copies = [pltpu.make_async_copy(s, t, sems.at[i]) for i, (s, t) in enumerate(zip(sources, targets))]
    for copy in copies:
        copy.start()
    return copies


def prepare_kernel(saved_hbm, incoming_hbm, occ_hbm, own_old, own_new, send_near, send_far, occ, saved, incoming, sems):
    even = (lax.axis_index("space") & 1) == 0
    copies = fetch((occ_hbm, saved_hbm, incoming_hbm), (occ, saved, incoming), sems)
    for copy in copies:
        copy.wait()
    occupied = occ[...].astype(F32).astype(BF16)
    for block in range(4):
        matrix = permutation(rows_mask(occupied, block))
        old = voxel_major(saved, block, matrix)
        new = voxel_major(incoming, block, matrix)
        part = slice(16 * block, 16 * block + 16)
        own_old[part] = old.astype(BF16)
        own_new[part] = new.astype(BF16)
        low = jnp.concatenate([old[:, :8], new[:, :8]], axis=1)
        high = jnp.concatenate([old[:, 8:], new[:, 8:]], axis=1)
        send_near[part] = jnp.where(even, high, low).astype(BF16)
        send_far[part] = jnp.where(even, low, high).astype(BF16)


def tables_kernel(
    cotangent_hbm, occ_hbm, neighbours_hbm, weight_hbm,
    own_grad, gather, gather_mixed, flipped, weight,
    occ, neighbours, cotangent, sems,
):
    index = lax.axis_index("space")
    even = (index & 1) == 0
    copies = fetch(
        (occ_hbm, neighbours_hbm, cotangent_hbm, weight_hbm), (occ, neighbours, cotangent, weight), sems
    )
    for copy in copies:
        copy.wait()
    occupied = occ[...].astype(F32).astype(BF16)
    for block in range(4):
        matrix = permutation(rows_mask(occupied, block))
        own_grad[16 * block : 16 * block + 16] = voxel_major(cotangent, block, matrix).astype(BF16)
    links = neighbours[...]
    near = links - index * 16
    high_base = jnp.where(even, 64, 128)
    low_base = jnp.where(even, 128, 64)
    outside = (near < 0) | (near >= 16)
    slot = jnp.where(near < 0, near + 8 + low_base, jnp.where(near < 16, near, near - 16 + high_base))
    lane = lax.broadcasted_iota(jnp.int32, (16, 192), 1)

    def one_hot(o, j, extra):
        target = slot[:, o : o + 1] + 16 * j
        if extra:
            target = target + jnp.where(outside[:, o : o + 1], 8, 0)
        target = jnp.where(links[:, o : o + 1] < 0, -1, target)
        return jnp.where(lane == target, 1.0, 0.0)

    for number, offsets in enumerate(MATRICES):
        for variant in range(2):
            rows = [one_hot(o, j, variant == 1) for j, o in enumerate(offsets)]
            gather[variant, number] = jnp.concatenate(rows, axis=0).astype(BF16)
    for place, number in enumerate(MIXED):
        rows = [one_hot(o, j, j >= 2) for j, o in enumerate(MATRICES[number])]
        gather_mixed[place] = jnp.concatenate(rows, axis=0).astype(BF16)
    for o in range(27):
        flipped[128 * o : 128 * o + 128] = weight[128 * (26 - o) : 128 * (27 - o)].T


def voxel_of(cell):
    return 16 * cell[0] + 4 * cell[1] + cell[2]


def fill(padded, own, near, far, gather, variant, gather_mixed=None):
    near = near.at[1 - (lax.axis_index("space") & 1)]
    for x in range(4):
        for y in range(4):
            u = 16 * x + 4 * y
            padded[x + 1, y + 1, 1:5] = own[u : u + 4]
    for number, cells in PLAN:
        sources = [c[2] for c in cells]
        if variant is None:
            halves = [s[1] >> 1 for s in sources]
            tiles = [8 * s[0] + (4 * s[1] + s[2]) % 8 for s in sources]
            if len(set(halves)) == 1:
                matrix = gather[halves[0], number]
            else:
                matrix = gather_mixed[MIXED.index(number)]
        else:
            tiles = [voxel_of(s) for s in sources]
            matrix = gather[variant, number]
        rows = [own[voxel_of(s)] for s in sources] + [near[t] for t in tiles] + [far[t] for t in tiles]
        picked = jnp.dot(matrix, jnp.concatenate(rows, axis=0), preferred_element_type=F32)
        picked = picked.astype(BF16).reshape(4, 16, 128)
        for j, c in enumerate(cells):
            padded[c[1]] = picked[j]


def convolve(padded, weight, x):
    windows = []
    for dx in range(3):
        for dy in range(3):
            for dz in range(3):
                windows.append(padded[x + dx, dy : dy + 4, dz : dz + 4].reshape(256, 128))
    return jnp.dot(jnp.concatenate(windows, axis=1), weight[...], preferred_element_type=F32)


def sigmoid(v):
    return 1.0 / (1.0 + jnp.exp(-v))


def old_kernel(own, near, far, own_grad, gather, weight, grad, send_near, send_far, padded):
    even = (lax.axis_index("space") & 1) == 0
    fill(padded, own, near, far, gather, 0)
    for x in range(4):
        v = convolve(padded, weight, x)
        q = sigmoid(v)
        slope = q * (1.0 + v * (1.0 - q))
        part = slice(16 * x, 16 * x + 16)
        value = own_grad[part].astype(F32) * slope.reshape(16, 16, 128)
        grad[part] = value.astype(BF16)
        low = jnp.concatenate([value[:8, :8], value[8:, :8]], axis=1)
        high = jnp.concatenate([value[:8, 8:], value[8:, 8:]], axis=1)
        here = slice(8 * x, 8 * x + 8)
        send_near[here] = jnp.where(even, high, low).astype(BF16)
        send_far[here] = jnp.where(even, low, high).astype(BF16)


def store_bricks(out, x, value, mask):
    matrix = permutation(mask[16 * x : 16 * x + 16])
    bricks = jnp.dot(matrix, value.astype(BF16), preferred_element_type=F32)
    out[:, 16 * x : 16 * x + 16] = bricks.astype(BF16).reshape(16, 16, 128)


def new_kernel(own, near, far, occ, gather, weight, out, padded):
    mask = columns_mask(occ[...].astype(F32).astype(BF16))
    fill(padded, own, near, far, gather, 1)
    for x in range(4):
        v = convolve(padded, weight, x)
        base = own[16 * x : 16 * x + 16].reshape(256, 128).astype(F32)
        store_bricks(out, x, base + v * sigmoid(v), mask)


def back_kernel(own, near, far, own_grad, occ, gather, gather_mixed, flipped, out, padded):
    mask = columns_mask(occ[...].astype(F32).astype(BF16))
    fill(padded, own, near, far, gather, None, gather_mixed)
    for x in range(4):
        v = convolve(padded, flipped, x)
        base = own_grad[16 * x : 16 * x + 16].reshape(256, 128).astype(F32)
        store_bricks(out, x, base + v, mask)


PADDED = pltpu.VMEM((6, 6, 6, 16, 128), BF16)
BRICKS = pltpu.VMEM((16, 64, 128), BF16)
OCC = pltpu.VMEM((16, 64), jnp.int32)
HBM = pl.BlockSpec(memory_space=pltpu.HBM)
VMEM = pl.BlockSpec(memory_space=pltpu.VMEM)


def call(kernel, shapes, ins, out, scratch=(), flops=0):
    place = pltpu.HBM if out is HBM else pltpu.VMEM
    run = pl.pallas_call(
        kernel,
        out_shape=[place(s, BF16) for s in shapes],
        in_specs=ins,
        out_specs=[out] * len(shapes),
        scratch_shapes=list(scratch),
        compiler_params=pltpu.CompilerParams(vmem_limit_bytes=VMEM_LIMIT),
        cost_estimate=pl.CostEstimate(flops=flops, bytes_accessed=2 << 20, transcendentals=0),
    )

    def placed(*arrays):
        spaces = [pltpu.HBM if spec is HBM else pltpu.VMEM for spec in ins]
        return run(*[pltpu.with_memory_space_constraint(a, m) for a, m in zip(arrays, spaces)])

    return placed


def across(value, count):
    pairs = [(i, i + 1) for i in range(1, count - 1, 2)]
    return lax.ppermute(value, "space", pairs + [(b, a) for a, b in pairs])


def inside(value, count):
    return lax.all_gather(value, "space", axis_index_groups=[[i, i + 1] for i in range(0, count, 2)])


def flush_kernel(source, out, sem):
    copy = pltpu.make_async_copy(source, out, sem)
    copy.start()
    copy.wait()


def per_device(count, sections, incoming, saved, cotangent, occupancy, neighbours, conv_weight):
    incoming, saved, cotangent, occ = incoming[0], saved[0], cotangent[0], occupancy[0]
    links, weight = neighbours[0], conv_weight[0].reshape(27 * 128, 128)
    tile = (64, 16, 128)
    half = (32, 16, 128)
    own_old, own_new, near, far = call(
        prepare_kernel, [tile] * 4, [HBM] * 3, VMEM, [OCC, BRICKS, BRICKS, pltpu.SemaphoreType.DMA((3,))]
    )(saved, incoming, occ)
    far = across(far, count)
    own_grad, gather, gather_mixed, flipped, flat = call(
        tables_kernel,
        [tile, (2, COUNT, 64, 192), (len(MIXED), 64, 192), (27 * 128, 128), (27 * 128, 128)],
        [HBM] * 4,
        VMEM,
        [OCC, pltpu.VMEM((16, 27), jnp.int32), BRICKS, pltpu.SemaphoreType.DMA((4,))],
        flops=1 << 31,
    )(cotangent, occ, links, weight)
    near, own_grad = lax.optimization_barrier((near, own_grad))
    near = inside(near, count)
    grad, grad_near, grad_far = call(
        old_kernel, [tile, half, half], [VMEM] * 6, VMEM, [PADDED], flops=1 << 30
    )(own_old, near, far, own_grad, gather, flat)
    grad_far = across(grad_far, count)
    grad_near = inside(grad_near, count)
    (out,) = call(new_kernel, [(16, 64, 128)], [VMEM] * 6, VMEM, [PADDED], flops=1 << 30)(
        own_new, near, far, occ, gather, flat
    )
    arrived = lax.ppermute(out[None], "segment", [(s, s + 1) for s in range(sections - 1)])
    (back,) = call(back_kernel, [(16, 64, 128)], [VMEM] * 8, VMEM, [PADDED], flops=1 << 30)(
        grad, grad_near, grad_far, own_grad, occ, gather, gather_mixed, flipped
    )
    returned = lax.ppermute(back[None], "segment", [(s + 1, s) for s in range(sections - 1)])
    (arrived,) = call(flush_kernel, [(1, 16, 64, 128)], [VMEM], HBM, [pltpu.SemaphoreType.DMA])(arrived)
    return arrived, returned


def solution(mesh):
    brick = P("segment", "space", None, None)
    index = P("segment", "space", None)
    return jax.shard_map(
        functools.partial(per_device, mesh.shape["space"], mesh.shape["segment"]),
        mesh=mesh,
        in_specs=(brick, brick, brick, index, index, P("segment", None, None, None)),
        out_specs=(brick, brick),
        check_vma=False,
    )
```

profile of v0, /device:TPU:198, one launch (start us, length us, event | category | flops | bytes accessed | tf_op | source)
XLA Modules:
  0.0 47.0 jit_solution(8959688668170722023)
XLA Ops:
  0.6 2.0 %shard_map.77 = (bf16[64,16,128]{2,1,0:T(8,128)(2,1)S(1)}, bf16[64,16,128]{2,1,0:T(8,128)(2,1)S(1)}, bf16[64,16,128]{2,1,0:T(8,128)(2,1)S(1)}, bf16[64,16,128]{2,1,0:T(8,128)(2,1)S(1)}) custom-call(bf16[16,64,128]{2,1,0:T(8,128)(2,1)} %bitcast.19, bf16[16,64,128]{2,1,0:T(8,128)(2,1)} %bitcast.20, s32[16,64]{1,0:T(8,128)} %bitcast.13), custom_call_target="tpu_custom_call" | custom-call | bytes 2097152 | tf_op jit(solution)/shard_map/pallas_call | solution.py:272
  2.6 5.1 %collective-permute-start = (bf16[64,16,128]{2,1,0:T(8,128)(2,1)S(1)}, bf16[64,16,128]{2,1,0:T(8,128)(2,1)S(1)}, u32[]{:S(2)}, u32[]{:S(2)}) collective-permute-start(bf16[64,16,128]{2,1,0:T(8,128)(2,1)S(1)} %get-tuple-element.20), channel_id=1, source_target_pairs={{12,24},{36,48},{60,72},{84,96},{108,120},{132,144},{156,168},{180... | collective-permute-start | bytes 786440 | tf_op jit(solution)/shard_map/ppermute | solution.py:279
  7.7 2.1 %shard_map.78 = (bf16[64,16,128]{2,1,0:T(8,128)(2,1)S(1)}, bf16[2,20,64,192]{3,2,1,0:T(8,128)(2,1)S(1)}, bf16[4,64,192]{2,1,0:T(8,128)(2,1)S(1)}, bf16[3456,128]{1,0:T(8,128)(2,1)S(1)}, bf16[3456,128]{1,0:T(8,128)(2,1)S(1)}) custom-call(bf16[16,64,128]{2,1,0:T(8,128)(2,1)} %bitcast.22, s32[16,64]{1,0:T(8,128)} %bitcast.14, s32[16,27]{1,0:T(8,128)} %bitcast.23, ...), custom_call_target="tpu_custom_call" | custom-call | flops 2147483648 | bytes 2097152 | tf_op jit(solution)/shard_map/pallas_call | solution.py:272
  9.8 2.2 %all-gather = bf16[128,16,128]{2,1,0:T(8,128)(2,1)S(1)} all-gather(bf16[64,16,128]{2,1,0:T(8,128)(2,1)S(1)} %get-tuple-element.19), channel_id=2, replica_groups={{0,12},{24,36},{48,60},{72,84},{96,108},{120,132},{144,156},{168,180},{..., dimensions={0}, use_global_device_ids=true | all-gather | bytes 786432 | tf_op jit(solution)/shard_map/all_gather | solution.py:283
  12.0 0.5 collective-permute-done.far
  12.4 0.0 copy-start
  12.4 2.8 %shard_map.81 = (bf16[64,16,128]{2,1,0:T(8,128)(2,1)S(1)}, bf16[32,16,128]{2,1,0:T(8,128)(2,1)S(1)}, bf16[32,16,128]{2,1,0:T(8,128)(2,1)S(1)}) custom-call(bf16[64,16,128]{2,1,0:T(8,128)(2,1)S(1)} %get-tuple-element.23.own, bf16[2,64,16,128]{3,2,1,0:T(8,128)(2,1)S(1)} %bitcast.10, bf16[64,16,128]{2,1,0:T(8,128)(2,1)S(1)} %collective-permute-done.far, ...), custom_call_target="tpu_custom_call" | custom-call | flops 1073741824 | bytes 2097152 | tf_op jit(solution)/shard_map/pallas_call | solution.py:272
  15.3 5.1 %collective-permute-start.2 = (bf16[32,16,128]{2,1,0:T(8,128)(2,1)S(1)}, bf16[32,16,128]{2,1,0:T(8,128)(2,1)S(1)}, u32[]{:S(2)}, u32[]{:S(2)}) collective-permute-start(bf16[32,16,128]{2,1,0:T(8,128)(2,1)S(1)} %get-tuple-element.27), channel_id=1, source_target_pairs={{12,24},{36,48},{60,72},{84,96},{108,120},{132,144},{156,168},{180... | collective-permute-start | bytes 393224 | tf_op jit(solution)/shard_map/ppermute | solution.py:279
  20.4 0.0 copy-done
  20.4 3.5 %shard_map.79 = bf16[16,64,128]{2,1,0:T(8,128)(2,1)S(1)} custom-call(bf16[64,16,128]{2,1,0:T(8,128)(2,1)S(1)} %get-tuple-element.16.own, bf16[2,64,16,128]{3,2,1,0:T(8,128)(2,1)S(1)} %bitcast.11, bf16[64,16,128]{2,1,0:T(8,128)(2,1)S(1)} %collective-permute-done.far, s32[16,64]{1,0:T(8,128)S(1)} %bitcast.15, ...), custom_call_target="tpu_custom_call" | custom-call | flops 1073741824 | bytes 2097152 | tf_op jit(solution)/shard_map/pallas_call | solution.py:272
  23.9 5.5 %collective-permute-start.1 = (bf16[1,16,64,128]{3,2,1,0:T(8,128)(2,1)S(1)}, bf16[1,16,64,128]{3,2,1,0:T(8,128)(2,1)S(1)}, u32[]{:S(2)}, u32[]{:S(2)}) collective-permute-start(bf16[1,16,64,128]{3,2,1,0:T(8,128)(2,1)S(1)} %bitcast.17), channel_id=1, source_target_pairs={{0,1},{1,2},{2,3},{3,4},{4,5},{5,6},{6,7},{7,8},{8,9},{9,10},{10,1... | collective-permute-start | bytes 786440 | tf_op jit(solution)/shard_map/ppermute | solution.py:319
  29.4 2.0 %all-gather.1 = bf16[64,16,128]{2,1,0:T(8,128)(2,1)S(1)} all-gather(bf16[32,16,128]{2,1,0:T(8,128)(2,1)S(1)} %get-tuple-element.26), channel_id=3, replica_groups={{0,12},{24,36},{48,60},{72,84},{96,108},{120,132},{144,156},{168,180},{..., dimensions={0}, use_global_device_ids=true | all-gather | bytes 393216 | tf_op jit(solution)/shard_map/all_gather | solution.py:283
  31.4 0.0 collective-permute-done.2.far
  31.4 3.5 %shard_map.82 = bf16[16,64,128]{2,1,0:T(8,128)(2,1)S(1)} custom-call(bf16[64,16,128]{2,1,0:T(8,128)(2,1)S(1)} %get-tuple-element.25.own, bf16[2,32,16,128]{3,2,1,0:T(8,128)(2,1)S(1)} %bitcast.12, bf16[32,16,128]{2,1,0:T(8,128)(2,1)S(1)} %collective-permute-done.2.far, bf16[64,16,128]{2,1,0:T(8,128)(2,1)S(1)} %get-tuple-element.24.own_grad, ...), custom_call_target="tpu_custom_call" | custom-call | flops 1073741824 | bytes 2097152 | tf_op jit(solution)/shard_map/pallas_call | solution.py:272
  34.9 1.9 %collective-permute-start.3 = (bf16[1,16,64,128]{3,2,1,0:T(8,128)(2,1)S(1)}, bf16[1,16,64,128]{3,2,1,0:T(8,128)(2,1)S(1)}, u32[]{:S(2)}, u32[]{:S(2)}) collective-permute-start(bf16[1,16,64,128]{3,2,1,0:T(8,128)(2,1)S(1)} %bitcast.18), channel_id=1, source_target_pairs={{1,0},{2,1},{3,2},{4,3},{5,4},{6,5},{7,6},{8,7},{9,8},{10,9},{11,1... | collective-permute-start | bytes 786440 | tf_op jit(solution)/shard_map/ppermute | solution.py:323
  36.8 0.0 collective-permute-done.1.source
  36.8 0.7 %shard_map.80 = bf16[1,16,64,128]{3,2,1,0:T(8,128)(2,1)} custom-call(bf16[1,16,64,128]{3,2,1,0:T(8,128)(2,1)S(1)} %collective-permute-done.1.source), custom_call_target="tpu_custom_call" | custom-call | bytes 2097152 | tf_op jit(solution)/shard_map/pallas_call | solution.py:272
  37.5 8.8 %collective-permute-done.3 = bf16[1,16,64,128]{3,2,1,0:T(8,128)(2,1)S(1)} collective-permute-done((bf16[1,16,64,128]{3,2,1,0:T(8,128)(2,1)S(1)}, bf16[1,16,64,128]{3,2,1,0:T(8,128)(2,1)S(1)}, u32[]{:S(2)}, u32[]{:S(2)}) %collective-permute-start.3) | collective-permute-done | bytes 262176 | tf_op jit(solution)/shard_map/ppermute | solution.py:323
  46.3 0.7 %copy.9 = bf16[1,16,64,128]{3,2,1,0:T(8,128)(2,1)} copy(bf16[1,16,64,128]{3,2,1,0:T(8,128)(2,1)S(1)} %collective-permute-done.3) | data formatting | bytes 524288
Async XLA Ops:
  2.6 9.8 %collective-permute-start = (bf16[64,16,128]{2,1,0:T(8,128)(2,1)S(1)}, bf16[64,16,128]{2,1,0:T(8,128)(2,1)S(1)}, u32[]{:S(2)}, u32[]{:S(2)}) collective-permute-start(bf16[64,16,128]{2,1,0:T(8,128)(2,1)S(1)} %get-tuple-element.20), channel_id=1, source_target_pairs={{12,24},{36,48},{60,72},{84,96},{108,120},{132,144},{156,168},{180... | collective-permute-start | bytes 786440 | tf_op jit(solution)/shard_map/ppermute | solution.py:279
  12.4 7.9 %copy-start = (s32[1,16,64]{2,1,0:T(8,128)S(1)}, s32[1,16,64]{2,1,0:T(8,128)}, u32[]{:S(2)}) copy-start(s32[1,16,64]{2,1,0:T(8,128)} %param.9) | copy-start | bytes 12292
  15.3 16.1 %collective-permute-start.2 = (bf16[32,16,128]{2,1,0:T(8,128)(2,1)S(1)}, bf16[32,16,128]{2,1,0:T(8,128)(2,1)S(1)}, u32[]{:S(2)}, u32[]{:S(2)}) collective-permute-start(bf16[32,16,128]{2,1,0:T(8,128)(2,1)S(1)} %get-tuple-element.27), channel_id=1, source_target_pairs={{12,24},{36,48},{60,72},{84,96},{108,120},{132,144},{156,168},{180... | collective-permute-start | bytes 393224 | tf_op jit(solution)/shard_map/ppermute | solution.py:279
  23.9 12.9 %collective-permute-start.1 = (bf16[1,16,64,128]{3,2,1,0:T(8,128)(2,1)S(1)}, bf16[1,16,64,128]{3,2,1,0:T(8,128)(2,1)S(1)}, u32[]{:S(2)}, u32[]{:S(2)}) collective-permute-start(bf16[1,16,64,128]{3,2,1,0:T(8,128)(2,1)S(1)} %bitcast.17), channel_id=1, source_target_pairs={{0,1},{1,2},{2,3},{3,4},{4,5},{5,6},{6,7},{7,8},{8,9},{9,10},{10,1... | collective-permute-start | bytes 786440 | tf_op jit(solution)/shard_map/ppermute | solution.py:319
  34.9 11.5 %collective-permute-start.3 = (bf16[1,16,64,128]{3,2,1,0:T(8,128)(2,1)S(1)}, bf16[1,16,64,128]{3,2,1,0:T(8,128)(2,1)S(1)}, u32[]{:S(2)}, u32[]{:S(2)}) collective-permute-start(bf16[1,16,64,128]{3,2,1,0:T(8,128)(2,1)S(1)} %bitcast.18), channel_id=1, source_target_pairs={{1,0},{2,1},{3,2},{4,3},{5,4},{6,5},{7,6},{8,7},{9,8},{10,9},{11,1... | collective-permute-start | bytes 786440 | tf_op jit(solution)/shard_map/ppermute | solution.py:323
where the time goes:
time: 47.4 us; the launch traced here: 47 us
  starting transfers between devices  17.6 us (37%)
  Pallas kernels  14.6 us (31%)
  waiting for transfers between devices  9.26 us (20%)
  blocking collectives  4.18 us (9%)
  between operations  0.73 us (2%)
  local copies, waits for them, and re-layouts  0.71 us (1%)
    pallas_call x6, Pallas kernels, placed(): run(*[pltpu.with_memory_space_constraint(a, m) for a, m in zip(arrays, sp...  14.6 us
    ppermute x2, starting transfers between devices, across(): return lax.ppermute(value, 'space', pairs + [(b, a) for a, b in pairs])  10.2 us
    ppermute x1, waiting for transfers between devices, per_device(): lax.ppermute(back[None], 'segment', [(s + 1, s) for s in range(sections -...  8.8 us
    ppermute x1, starting transfers between devices, per_device(): lax.ppermute(out[None], 'segment', [(s, s + 1) for s in range(sections -...  5.49 us
    all_gather x2, blocking collectives, inside(): lax.all_gather(value, 'space', axis_index_groups=[[i, i + 1] for i in ran...  4.18 us
    ppermute x1, starting transfers between devices, per_device(): lax.ppermute(back[None], 'segment', [(s + 1, s) for s in range(sections -...  1.92 us
  transfers between devices with their start and end apart: 4, of which 2 were waited for; matrix products, arithmetic and copies ran while one was open for 0% of the time, Pallas kernels for 21%

commit v1 on v0

v1 whole, which is shorter than its diff:
```python
import functools

import jax
import jax.numpy as jnp
from jax import lax
from jax.experimental import pallas as pl
from jax.experimental.pallas import tpu as pltpu
from jax.sharding import PartitionSpec as P

BF16 = jnp.bfloat16
F32 = jnp.float32
STEPS = (-1, 0, 1)
VMEM_LIMIT = 40 * 1024 * 1024


def source_coordinate(step, c):
    return c if step == 0 else (3 if step < 0 else 0)


def padded_coordinate(step, c):
    return c + 1 if step == 0 else (0 if step < 0 else 5)


def offset_index(ex, ey, ez):
    return 9 * (ex + 1) + 3 * (ey + 1) + (ez + 1)


def gather_plan():
    matrices, plan, mixed = [], [], []
    corners = {-1: [], 1: []}
    for ex in STEPS:
        for ey in STEPS:
            for ez in STEPS:
                steps = (ex, ey, ez)
                zeros = [a for a in range(3) if steps[a] == 0]
                if len(zeros) == 3:
                    continue
                o = offset_index(ex, ey, ez)

                def cell(c):
                    source = [source_coordinate(s, v) for s, v in zip(steps, c)]
                    padded = [padded_coordinate(s, v) for s, v in zip(steps, c)]
                    return (o, tuple(padded), tuple(source))

                if not zeros:
                    corners[ey].append(cell((0, 0, 0)))
                    continue
                along = zeros[0] if len(zeros) == 1 else max(a for a in zeros if a != 1)
                index = len(matrices)
                matrices.append((o,) * 4)
                if along == 1:
                    mixed.append(index)
                outer = [a for a in zeros if a != along]
                groups = []
                for first in range(4) if outer else (0,):
                    cells = []
                    for second in range(4):
                        c = [0, 0, 0]
                        c[along] = second
                        if outer:
                            c[outer[0]] = first
                        cells.append(cell(c))
                    groups.append(cells)
                plan.append((index, groups))
    for ey in (-1, 1):
        plan.append((len(matrices), [corners[ey]]))
        matrices.append(tuple(c[0] for c in corners[ey]))
    return matrices, plan, mixed


MATRICES, PLAN, MIXED = gather_plan()
COUNT = len(MATRICES)


def voxel_major(ref, mask, block):
    part = slice(16 * block, 16 * block + 16)
    return jnp.swapaxes(ref[:, part, :].astype(F32), 0, 1) * mask[part].astype(F32)


def fetch(sources, targets, sems):
    copies = [pltpu.make_async_copy(s, t, sems.at[i]) for i, (s, t) in enumerate(zip(sources, targets))]
    for copy in copies:
        copy.start()
    return copies


def prepare_kernel(saved_hbm, incoming_hbm, occ_hbm, own_old, own_new, send_near, send_far, mask, occ, saved, incoming, sems):
    even = (lax.axis_index("space") & 1) == 0
    copies = fetch((occ_hbm, saved_hbm, incoming_hbm), (occ, saved, incoming), sems)
    copies[0].wait()
    occupied = occ[...].astype(F32)
    for u in range(64):
        mask[u] = jnp.broadcast_to(occupied[:, u : u + 1], (16, 128)).astype(BF16)
    copies[1].wait()
    copies[2].wait()
    for block in range(4):
        old = voxel_major(saved, mask, block)
        new = voxel_major(incoming, mask, block)
        part = slice(16 * block, 16 * block + 16)
        own_old[part] = old.astype(BF16)
        own_new[part] = new.astype(BF16)
        low = jnp.concatenate([old[:, :8], new[:, :8]], axis=1)
        high = jnp.concatenate([old[:, 8:], new[:, 8:]], axis=1)
        send_near[part] = jnp.where(even, high, low).astype(BF16)
        send_far[part] = jnp.where(even, low, high).astype(BF16)


def widened(out, kernel_of):
    for k in range(9):
        blocks = [kernel_of(3 * k + i) for i in range(3)]
        zero = jnp.zeros_like(blocks[0])
        for j in range(4):
            row = slice(128 * (4 * k + j), 128 * (4 * k + j + 1))
            out[row, :128] = blocks[j] if j < 3 else zero
            out[row, 128:] = blocks[j - 1] if j > 0 else zero


def tables_kernel(
    cotangent_hbm, neighbours_hbm, weight_hbm, mask,
    own_grad, gather, gather_mixed, wide, flipped,
    neighbours, cotangent, weight, sems,
):
    index = lax.axis_index("space")
    even = (index & 1) == 0
    copies = fetch(
        (neighbours_hbm, cotangent_hbm, weight_hbm), (neighbours, cotangent, weight), sems
    )
    copies[0].wait()
    links = neighbours[...]
    near = links - index * 16
    high_base = jnp.where(even, 64, 128)
    low_base = jnp.where(even, 128, 64)
    outside = (near < 0) | (near >= 16)
    slot = jnp.where(near < 0, near + 8 + low_base, jnp.where(near < 16, near, near - 16 + high_base))
    slot = jnp.where(links < 0, -1024, slot)
    moved = jnp.where(outside, slot + 8, slot)
    lane = lax.broadcasted_iota(jnp.int32, (64, 192), 1) - 16 * (
        lax.broadcasted_iota(jnp.int32, (64, 192), 0) >> 4
    )

    def one_hot(offsets, extra):
        columns = [(moved if e else slot)[:, o : o + 1] for o, e in zip(offsets, extra)]
        return jnp.where(lane == jnp.concatenate(columns, axis=0), 1.0, 0.0).astype(BF16)

    for number, offsets in enumerate(MATRICES):
        gather[0, number] = one_hot(offsets, (False,) * 4)
        gather[1, number] = one_hot(offsets, (True,) * 4)
    for place, number in enumerate(MIXED):
        gather_mixed[place] = one_hot(MATRICES[number], (False, False, True, True))
    copies[1].wait()
    for block in range(4):
        own_grad[16 * block : 16 * block + 16] = voxel_major(cotangent, mask, block).astype(BF16)
    copies[2].wait()
    widened(wide, lambda o: weight[o])
    widened(flipped, lambda o: weight[26 - o].T)


def voxel_of(cell):
    return 16 * cell[0] + 4 * cell[1] + cell[2]


def fill(padded, own, near, far, gather, variant, gather_mixed=None):
    near = near.at[1 - (lax.axis_index("space") & 1)]
    for x in range(4):
        for y in range(4):
            u = 16 * x + 4 * y
            padded[x + 1, y + 1, 1:5] = own[u : u + 4]
    for number, groups in PLAN:
        columns = []
        for cells in groups:
            sources = [c[2] for c in cells]
            tiles = [voxel_of(s) for s in sources]
            if variant is None:
                halves = [s[1] >> 1 for s in sources]
                tiles = [8 * s[0] + (4 * s[1] + s[2]) % 8 for s in sources]
            rows = [own[voxel_of(s)] for s in sources] + [near[t] for t in tiles] + [far[t] for t in tiles]
            columns.append((jnp.concatenate(rows, axis=0), halves if variant is None else [variant] * 4, cells))
        kinds = sorted({tuple(c[1]) for c in columns})
        for kind in kinds:
            chosen = [c for c in columns if tuple(c[1]) == kind]
            matrix = gather[kind[0], number] if len(set(kind)) == 1 else gather_mixed[MIXED.index(number)]
            picked = jnp.dot(
                matrix, jnp.concatenate([c[0] for c in chosen], axis=1), preferred_element_type=F32
            ).astype(BF16)
            for i, (_, _, cells) in enumerate(chosen):
                part = picked[:, 128 * i : 128 * i + 128].reshape(4, 16, 128)
                for j, c in enumerate(cells):
                    padded[c[1]] = part[j]


def convolve(padded, weight, x):
    windows = []
    for dx in range(3):
        for dy in range(3):
            for j in range(4):
                windows.append(padded[x + dx : x + dx + 2, dy : dy + 4, j : j + 3 : 2].reshape(256, 128))
    both = jnp.dot(jnp.concatenate(windows, axis=1), weight[...], preferred_element_type=F32)
    halves = [both[:, 128 * h : 128 * h + 128].reshape(16, 1, 16, 128) for h in range(2)]
    return jnp.concatenate(halves, axis=1).reshape(32, 16, 128)


def sigmoid(v):
    return 1.0 / (1.0 + jnp.exp(-v))


def old_kernel(own, near, far, own_grad, gather, weight, grad, send_near, send_far, padded):
    even = (lax.axis_index("space") & 1) == 0
    fill(padded, own, near, far, gather, 0)
    for pair in range(2):
        v = convolve(padded, weight, 2 * pair)
        q = sigmoid(v)
        slope = q * (1.0 + v * (1.0 - q))
        part = slice(32 * pair, 32 * pair + 32)
        value = own_grad[part].astype(F32) * slope
        grad[part] = value.astype(BF16)
        for h in range(2):
            first, second = value[16 * h : 16 * h + 8], value[16 * h + 8 : 16 * h + 16]
            low = jnp.concatenate([first[:, :8], second[:, :8]], axis=1)
            high = jnp.concatenate([first[:, 8:], second[:, 8:]], axis=1)
            here = slice(16 * pair + 8 * h, 16 * pair + 8 * h + 8)
            send_near[here] = jnp.where(even, high, low).astype(BF16)
            send_far[here] = jnp.where(even, low, high).astype(BF16)


def store_bricks(out, pair, value, mask):
    part = slice(32 * pair, 32 * pair + 32)
    out[:, part] = jnp.swapaxes(value * mask[part].astype(F32), 0, 1).astype(BF16)


def new_kernel(own, near, far, mask, gather, weight, out, padded):
    fill(padded, own, near, far, gather, 1)
    for pair in range(2):
        v = convolve(padded, weight, 2 * pair)
        base = own[32 * pair : 32 * pair + 32].astype(F32)
        store_bricks(out, pair, base + v * sigmoid(v), mask)


def back_kernel(own, near, far, own_grad, mask, gather, gather_mixed, flipped, out, padded):
    fill(padded, own, near, far, gather, None, gather_mixed)
    for pair in range(2):
        v = convolve(padded, flipped, 2 * pair)
        base = own_grad[32 * pair : 32 * pair + 32].astype(F32)
        store_bricks(out, pair, base + v, mask)


PADDED = pltpu.VMEM((6, 6, 6, 16, 128), BF16)
BRICKS = pltpu.VMEM((16, 64, 128), BF16)
OCC = pltpu.VMEM((16, 64), jnp.int32)
HBM = pl.BlockSpec(memory_space=pltpu.HBM)
VMEM = pl.BlockSpec(memory_space=pltpu.VMEM)


def call(kernel, shapes, ins, out, scratch=(), flops=0):
    place = pltpu.HBM if out is HBM else pltpu.VMEM
    run = pl.pallas_call(
        kernel,
        out_shape=[place(s, BF16) for s in shapes],
        in_specs=ins,
        out_specs=[out] * len(shapes),
        scratch_shapes=list(scratch),
        compiler_params=pltpu.CompilerParams(vmem_limit_bytes=VMEM_LIMIT),
        cost_estimate=pl.CostEstimate(flops=flops, bytes_accessed=2 << 20, transcendentals=0),
    )

    def placed(*arrays):
        spaces = [pltpu.HBM if spec is HBM else pltpu.VMEM for spec in ins]
        return run(*[pltpu.with_memory_space_constraint(a, m) for a, m in zip(arrays, spaces)])

    return placed


def across(value, count):
    pairs = [(i, i + 1) for i in range(1, count - 1, 2)]
    return lax.ppermute(value, "space", pairs + [(b, a) for a, b in pairs])


def inside(value, count):
    return lax.all_gather(value, "space", axis_index_groups=[[i, i + 1] for i in range(0, count, 2)])


def flush_kernel(source, out, sem):
    copy = pltpu.make_async_copy(source, out, sem)
    copy.start()
    copy.wait()


def per_device(count, sections, incoming, saved, cotangent, occupancy, neighbours, conv_weight):
    incoming, saved, cotangent, occ = incoming[0], saved[0], cotangent[0], occupancy[0]
    links, weight = neighbours[0], conv_weight[0]
    tile = (64, 16, 128)
    half = (32, 16, 128)
    own_old, own_new, near, far, mask = call(
        prepare_kernel, [tile] * 5, [HBM] * 3, VMEM, [OCC, BRICKS, BRICKS, pltpu.SemaphoreType.DMA((3,))]
    )(saved, incoming, occ)
    far = across(far, count)
    own_grad, gather, gather_mixed, wide, flipped = call(
        tables_kernel,
        [tile, (2, COUNT, 64, 192), (len(MIXED), 64, 192), (36 * 128, 256), (36 * 128, 256)],
        [HBM] * 3 + [VMEM],
        VMEM,
        [
            pltpu.VMEM((16, 27), jnp.int32),
            BRICKS,
            pltpu.VMEM((27, 128, 128), BF16),
            pltpu.SemaphoreType.DMA((3,)),
        ],
        flops=1 << 31,
    )(cotangent, links, weight, mask)
    near, own_grad = lax.optimization_barrier((near, own_grad))
    near = inside(near, count)
    grad, grad_near, grad_far = call(
        old_kernel, [tile, half, half], [VMEM] * 6, VMEM, [PADDED], flops=1 << 30
    )(own_old, near, far, own_grad, gather, wide)
    grad_far = across(grad_far, count)
    grad_near = inside(grad_near, count)
    (out,) = call(new_kernel, [(16, 64, 128)], [VMEM] * 6, VMEM, [PADDED], flops=1 << 30)(
        own_new, near, far, mask, gather, wide
    )
    arrived = lax.ppermute(out[None], "segment", [(s, s + 1) for s in range(sections - 1)])
    (back,) = call(back_kernel, [(16, 64, 128)], [VMEM] * 8, VMEM, [PADDED], flops=1 << 30)(
        grad, grad_near, grad_far, own_grad, mask, gather, gather_mixed, flipped
    )
    returned = lax.ppermute(back[None], "segment", [(s + 1, s) for s in range(sections - 1)])
    (arrived,) = call(flush_kernel, [(1, 16, 64, 128)], [VMEM], HBM, [pltpu.SemaphoreType.DMA])(arrived)
    return arrived, returned


def solution(mesh):
    brick = P("segment", "space", None, None)
    index = P("segment", "space", None)
    return jax.shard_map(
        functools.partial(per_device, mesh.shape["space"], mesh.shape["segment"]),
        mesh=mesh,
        in_specs=(brick, brick, brick, index, index, P("segment", None, None, None)),
        out_specs=(brick, brick),
        check_vma=False,
    )
```

time: 47.4 us -> 43 us (0.907)
  Pallas kernels: 14.6 us -> 10.1 us
    pallas_call x6, Pallas kernels: 14.6 us -> 10.1 us  [placed(): run(*[pltpu.with_memory_space_constraint(a, m) for a, m in zip(arrays, sp...]
  transfers between devices with their start and end apart: 4 -> 4, of which waited for: 2 -> 2; matrix products, arithmetic and copies ran while one was open for 0% -> 0% of each run, Pallas kernels for 21% -> 16%
where the time goes in v1:
time: 43 us; the launch traced here: 42.7 us
  starting transfers between devices  17.6 us (41%)
  Pallas kernels  10.1 us (23%)
  waiting for transfers between devices  9.4 us (22%)
  blocking collectives  4.18 us (10%)
  between operations  0.72 us (2%)
  local copies, waits for them, and re-layouts  0.7 us (2%)
    ppermute x2, starting transfers between devices, across(): return lax.ppermute(value, 'space', pairs + [(b, a) for a, b in pairs])  10.2 us
    pallas_call x6, Pallas kernels, placed(): run(*[pltpu.with_memory_space_constraint(a, m) for a, m in zip(arrays, sp...  10.1 us
    ppermute x1, waiting for transfers between devices, per_device(): lax.ppermute(back[None], 'segment', [(s + 1, s) for s in range(sections -...  8.8 us
    ppermute x1, starting transfers between devices, per_device(): lax.ppermute(out[None], 'segment', [(s, s + 1) for s in range(sections -...  5.49 us
    all_gather x2, blocking collectives, inside(): lax.all_gather(value, 'space', axis_index_groups=[[i, i + 1] for i in ran...  4.18 us
    ppermute x1, starting transfers between devices, per_device(): lax.ppermute(back[None], 'segment', [(s + 1, s) for s in range(sections -...  1.92 us
  transfers between devices with their start and end apart: 4, of which 2 were waited for; matrix products, arithmetic and copies ran while one was open for 0% of the time, Pallas kernels for 16%

profile of v1, /device:TPU:198, one launch (start us, length us, event | category | flops | bytes accessed | tf_op | source)
XLA Modules:
  0.0 42.7 jit_solution(172102228920675319)
XLA Ops:
  0.6 1.5 %shard_map.77 = (bf16[64,16,128]{2,1,0:T(8,128)(2,1)S(1)}, bf16[64,16,128]{2,1,0:T(8,128)(2,1)S(1)}, bf16[64,16,128]{2,1,0:T(8,128)(2,1)S(1)}, bf16[64,16,128]{2,1,0:T(8,128)(2,1)S(1)}, bf16[64,16,128]{2,1,0:T(8,128)(2,1)S(1)}) custom-call(bf16[16,64,128]{2,1,0:T(8,128)(2,1)} %bitcast.15, bf16[16,64,128]{2,1,0:T(8,128)(2,1)} %bitcast.16, s32[16,64]{1,0:T(8,128)} %bitcast.17), custom_call_target="tpu_custom_call" | custom-call | bytes 2097152 | tf_op jit(solution)/shard_map/pallas_call | solution.py:267
  2.1 5.1 %collective-permute-start = (bf16[64,16,128]{2,1,0:T(8,128)(2,1)S(1)}, bf16[64,16,128]{2,1,0:T(8,128)(2,1)S(1)}, u32[]{:S(2)}, u32[]{:S(2)}) collective-permute-start(bf16[64,16,128]{2,1,0:T(8,128)(2,1)S(1)} %get-tuple-element.22), channel_id=1, source_target_pairs={{12,24},{36,48},{60,72},{84,96},{108,120},{132,144},{156,168},{180... | collective-permute-start | bytes 786440 | tf_op jit(solution)/shard_map/ppermute | solution.py:274
  7.2 1.9 %shard_map.78 = (bf16[64,16,128]{2,1,0:T(8,128)(2,1)S(1)}, bf16[2,20,64,192]{3,2,1,0:T(8,128)(2,1)S(1)}, bf16[4,64,192]{2,1,0:T(8,128)(2,1)S(1)}, bf16[4608,256]{1,0:T(8,128)(2,1)S(1)}, bf16[4608,256]{1,0:T(8,128)(2,1)S(1)}) custom-call(bf16[16,64,128]{2,1,0:T(8,128)(2,1)} %bitcast.19, s32[16,27]{1,0:T(8,128)} %bitcast.20, bf16[27,128,128]{2,1,0:T(8,128)(2,1)} %bitcast.18, ...), custom_call_target="tpu_custom_call" | custom-call | flops 2147483648 | bytes 2097152 | tf_op jit(solution)/shard_map/pallas_call | solution.py:267
  9.1 2.2 %all-gather = bf16[128,16,128]{2,1,0:T(8,128)(2,1)S(1)} all-gather(bf16[64,16,128]{2,1,0:T(8,128)(2,1)S(1)} %get-tuple-element.21), channel_id=2, replica_groups={{0,12},{24,36},{48,60},{72,84},{96,108},{120,132},{144,156},{168,180},{..., dimensions={0}, use_global_device_ids=true | all-gather | bytes 786432 | tf_op jit(solution)/shard_map/all_gather | solution.py:278
  11.3 0.6 %collective-permute-done.far = bf16[64,16,128]{2,1,0:T(8,128)(2,1)S(1)} collective-permute-done((bf16[64,16,128]{2,1,0:T(8,128)(2,1)S(1)}, bf16[64,16,128]{2,1,0:T(8,128)(2,1)S(1)}, u32[]{:S(2)}, u32[]{:S(2)}) %collective-permute-start) | collective-permute-done | bytes 262176 | tf_op jit(solution)/shard_map/ppermute | solution.py:274
  11.9 2.0 %shard_map.81 = (bf16[64,16,128]{2,1,0:T(8,128)(2,1)S(1)}, bf16[32,16,128]{2,1,0:T(8,128)(2,1)S(1)}, bf16[32,16,128]{2,1,0:T(8,128)(2,1)S(1)}) custom-call(bf16[64,16,128]{2,1,0:T(8,128)(2,1)S(1)} %get-tuple-element.25.own, bf16[2,64,16,128]{3,2,1,0:T(8,128)(2,1)S(1)} %bitcast.10, bf16[64,16,128]{2,1,0:T(8,128)(2,1)S(1)} %collective-permute-done.far, ...), custom_call_target="tpu_custom_call" | custom-call | flops 1073741824 | bytes 2097152 | tf_op jit(solution)/shard_map/pallas_call | solution.py:267
  13.9 5.1 %collective-permute-start.2 = (bf16[32,16,128]{2,1,0:T(8,128)(2,1)S(1)}, bf16[32,16,128]{2,1,0:T(8,128)(2,1)S(1)}, u32[]{:S(2)}, u32[]{:S(2)}) collective-permute-start(bf16[32,16,128]{2,1,0:T(8,128)(2,1)S(1)} %get-tuple-element.29), channel_id=1, source_target_pairs={{12,24},{36,48},{60,72},{84,96},{108,120},{132,144},{156,168},{180... | collective-permute-start | bytes 393224 | tf_op jit(solution)/shard_map/ppermute | solution.py:274
  19.0 2.1 %shard_map.79 = bf16[16,64,128]{2,1,0:T(8,128)(2,1)S(1)} custom-call(bf16[64,16,128]{2,1,0:T(8,128)(2,1)S(1)} %get-tuple-element.17.own, bf16[2,64,16,128]{3,2,1,0:T(8,128)(2,1)S(1)} %bitcast.11, bf16[64,16,128]{2,1,0:T(8,128)(2,1)S(1)} %collective-permute-done.far, bf16[64,16,128]{2,1,0:T(8,128)(2,1)S(1)} %get-tuple-element.19.mask, ...), custom_call_target="tpu_custom_call" | custom-call | flops 1073741824 | bytes 2097152 | tf_op jit(solution)/shard_map/pallas_call | solution.py:267
  21.1 5.5 %collective-permute-start.1 = (bf16[1,16,64,128]{3,2,1,0:T(8,128)(2,1)S(1)}, bf16[1,16,64,128]{3,2,1,0:T(8,128)(2,1)S(1)}, u32[]{:S(2)}, u32[]{:S(2)}) collective-permute-start(bf16[1,16,64,128]{3,2,1,0:T(8,128)(2,1)S(1)} %bitcast.13), channel_id=1, source_target_pairs={{0,1},{1,2},{2,3},{3,4},{4,5},{5,6},{6,7},{7,8},{8,9},{9,10},{10,1... | collective-permute-start | bytes 786440 | tf_op jit(solution)/shard_map/ppermute | solution.py:319
  26.6 2.0 %all-gather.1 = bf16[64,16,128]{2,1,0:T(8,128)(2,1)S(1)} all-gather(bf16[32,16,128]{2,1,0:T(8,128)(2,1)S(1)} %get-tuple-element.28), channel_id=3, replica_groups={{0,12},{24,36},{48,60},{72,84},{96,108},{120,132},{144,156},{168,180},{..., dimensions={0}, use_global_device_ids=true | all-gather | bytes 393216 | tf_op jit(solution)/shard_map/all_gather | solution.py:278
  28.6 0.0 collective-permute-done.2.far
  28.6 1.9 %shard_map.82 = bf16[16,64,128]{2,1,0:T(8,128)(2,1)S(1)} custom-call(bf16[64,16,128]{2,1,0:T(8,128)(2,1)S(1)} %get-tuple-element.27.own, bf16[2,32,16,128]{3,2,1,0:T(8,128)(2,1)S(1)} %bitcast.12, bf16[32,16,128]{2,1,0:T(8,128)(2,1)S(1)} %collective-permute-done.2.far, bf16[64,16,128]{2,1,0:T(8,128)(2,1)S(1)} %get-tuple-element.26.own_grad, ...), custom_call_target="tpu_custom_call" | custom-call | flops 1073741824 | bytes 2097152 | tf_op jit(solution)/shard_map/pallas_call | solution.py:267
  30.5 1.9 %collective-permute-start.3 = (bf16[1,16,64,128]{3,2,1,0:T(8,128)(2,1)S(1)}, bf16[1,16,64,128]{3,2,1,0:T(8,128)(2,1)S(1)}, u32[]{:S(2)}, u32[]{:S(2)}) collective-permute-start(bf16[1,16,64,128]{3,2,1,0:T(8,128)(2,1)S(1)} %bitcast.14), channel_id=1, source_target_pairs={{1,0},{2,1},{3,2},{4,3},{5,4},{6,5},{7,6},{8,7},{9,8},{10,9},{11,1... | collective-permute-start | bytes 786440 | tf_op jit(solution)/shard_map/ppermute | solution.py:323
  32.4 0.0 collective-permute-done.1.source
  32.5 0.7 %shard_map.80 = bf16[1,16,64,128]{3,2,1,0:T(8,128)(2,1)} custom-call(bf16[1,16,64,128]{3,2,1,0:T(8,128)(2,1)S(1)} %collective-permute-done.1.source), custom_call_target="tpu_custom_call" | custom-call | bytes 2097152 | tf_op jit(solution)/shard_map/pallas_call | solution.py:267
  33.2 8.8 %collective-permute-done.3 = bf16[1,16,64,128]{3,2,1,0:T(8,128)(2,1)S(1)} collective-permute-done((bf16[1,16,64,128]{3,2,1,0:T(8,128)(2,1)S(1)}, bf16[1,16,64,128]{3,2,1,0:T(8,128)(2,1)S(1)}, u32[]{:S(2)}, u32[]{:S(2)}) %collective-permute-start.3) | collective-permute-done | bytes 262176 | tf_op jit(solution)/shard_map/ppermute | solution.py:323
  42.0 0.7 %copy.9 = bf16[1,16,64,128]{3,2,1,0:T(8,128)(2,1)} copy(bf16[1,16,64,128]{3,2,1,0:T(8,128)(2,1)S(1)} %collective-permute-done.3) | data formatting | bytes 524288
Async XLA Ops:
  2.1 9.8 %collective-permute-start = (bf16[64,16,128]{2,1,0:T(8,128)(2,1)S(1)}, bf16[64,16,128]{2,1,0:T(8,128)(2,1)S(1)}, u32[]{:S(2)}, u32[]{:S(2)}) collective-permute-start(bf16[64,16,128]{2,1,0:T(8,128)(2,1)S(1)} %get-tuple-element.22), channel_id=1, source_target_pairs={{12,24},{36,48},{60,72},{84,96},{108,120},{132,144},{156,168},{180... | collective-permute-start | bytes 786440 | tf_op jit(solution)/shard_map/ppermute | solution.py:274
  13.9 14.7 %collective-permute-start.2 = (bf16[32,16,128]{2,1,0:T(8,128)(2,1)S(1)}, bf16[32,16,128]{2,1,0:T(8,128)(2,1)S(1)}, u32[]{:S(2)}, u32[]{:S(2)}) collective-permute-start(bf16[32,16,128]{2,1,0:T(8,128)(2,1)S(1)} %get-tuple-element.29), channel_id=1, source_target_pairs={{12,24},{36,48},{60,72},{84,96},{108,120},{132,144},{156,168},{180... | collective-permute-start | bytes 393224 | tf_op jit(solution)/shard_map/ppermute | solution.py:274
  21.1 11.4 %collective-permute-start.1 = (bf16[1,16,64,128]{3,2,1,0:T(8,128)(2,1)S(1)}, bf16[1,16,64,128]{3,2,1,0:T(8,128)(2,1)S(1)}, u32[]{:S(2)}, u32[]{:S(2)}) collective-permute-start(bf16[1,16,64,128]{3,2,1,0:T(8,128)(2,1)S(1)} %bitcast.13), channel_id=1, source_target_pairs={{0,1},{1,2},{2,3},{3,4},{4,5},{5,6},{6,7},{7,8},{8,9},{9,10},{10,1... | collective-permute-start | bytes 786440 | tf_op jit(solution)/shard_map/ppermute | solution.py:319
  30.5 11.5 %collective-permute-start.3 = (bf16[1,16,64,128]{3,2,1,0:T(8,128)(2,1)S(1)}, bf16[1,16,64,128]{3,2,1,0:T(8,128)(2,1)S(1)}, u32[]{:S(2)}, u32[]{:S(2)}) collective-permute-start(bf16[1,16,64,128]{3,2,1,0:T(8,128)(2,1)S(1)} %bitcast.14), channel_id=1, source_target_pairs={{1,0},{2,1},{3,2},{4,3},{5,4},{6,5},{7,6},{8,7},{9,8},{10,9},{11,1... | collective-permute-start | bytes 786440 | tf_op jit(solution)/shard_map/ppermute | solution.py:323

commit v2 on v1

v2 whole, which is shorter than its diff:
```python
import functools

import jax
import jax.numpy as jnp
from jax import lax
from jax.experimental import pallas as pl
from jax.experimental.pallas import tpu as pltpu
from jax.sharding import PartitionSpec as P

BF16 = jnp.bfloat16
F32 = jnp.float32
STEPS = (-1, 0, 1)
VMEM_LIMIT = 40 * 1024 * 1024


def source_coordinate(step, c):
    return c if step == 0 else (3 if step < 0 else 0)


def padded_coordinate(step, c):
    return c + 1 if step == 0 else (0 if step < 0 else 5)


def gather_plan():
    matrices, plan = [], []
    corners = {-1: [], 1: []}
    centre = None
    for o in range(27):
        steps = (o // 9 - 1, o // 3 % 3 - 1, o % 3 - 1)
        zeros = [a for a in range(3) if steps[a] == 0]

        def cell(c):
            source = [source_coordinate(s, v) for s, v in zip(steps, c)]
            padded = [padded_coordinate(s, v) for s, v in zip(steps, c)]
            return tuple(padded), 16 * source[0] + 4 * source[1] + source[2]

        if not zeros:
            corners[steps[1]].append((o, cell((0, 0, 0))))
            continue
        along, outer = zeros[-1], zeros[:-1]
        groups = []
        for first in range(4 ** len(outer)):
            c = [0, 0, 0]
            for a in outer:
                c[a] = first % 4
                first //= 4
            cells = []
            for second in range(4):
                c[along] = second
                cells.append(cell(c))
            groups.append(cells)
        if len(zeros) == 3:
            centre = ((o,) * 4, groups)
        else:
            matrices.append((o,) * 4)
            plan.append(groups)
    for side in (-1, 1):
        matrices.append(tuple(o for o, _ in corners[side]))
        plan.append([[c for _, c in corners[side]]])
    matrices.append(centre[0])
    plan.append(centre[1])
    return matrices, plan


MATRICES, PLAN = gather_plan()
COUNT = len(MATRICES)
LINKS = 128


def fetch(sources, targets, sems):
    copies = [pltpu.make_async_copy(s, t, sems.at[i]) for i, (s, t) in enumerate(zip(sources, targets))]
    for copy in copies:
        copy.start()
    return copies


def is_even():
    return (lax.axis_index("space") & 1) == 0


def voxel_major(ref, mask, block):
    part = slice(16 * block, 16 * block + 16)
    return jnp.swapaxes(ref[:, part, :].astype(F32), 0, 1) * mask[part].astype(F32)


def prepare_kernel(
    saved_hbm, cotangent_hbm, incoming_hbm, occ_hbm, links_hbm,
    send_near, send_far, own_new, own_grad, mask,
    occ, links, saved, cotangent, incoming, sems,
):
    even = is_even()
    copies = fetch(
        (occ_hbm, links_hbm, saved_hbm, cotangent_hbm, incoming_hbm), (occ, links, saved, cotangent, incoming), sems
    )
    copies[0].wait()
    occupied = occ[...].astype(F32)
    for u in range(64):
        mask[u] = jnp.broadcast_to(occupied[:, u : u + 1], (16, 128)).astype(BF16)
    copies[1].wait()
    named = links[...]
    first = 16 * lax.axis_index("space") + lax.broadcasted_iota(jnp.int32, (16, 27), 0)
    code = jnp.where(named < 0, 0, named - first + 8).astype(F32)
    code = jnp.concatenate([code, jnp.zeros((16, 101), F32)], axis=1).astype(BF16)
    send_near[LINKS] = code
    send_far[LINKS] = code
    for copy in copies[2:]:
        copy.wait()
    for block in range(4):
        part = slice(16 * block, 16 * block + 16)
        after = slice(64 + 16 * block, 64 + 16 * block + 16)
        old = voxel_major(saved, mask, block).astype(BF16)
        send_near[part] = old
        send_far[part] = old
        grad = voxel_major(cotangent, mask, block)
        new = voxel_major(incoming, mask, block)
        own_grad[part] = grad.astype(BF16)
        own_new[part] = new.astype(BF16)
        low = jnp.concatenate([grad[:, :8], new[:, :8]], axis=1)
        high = jnp.concatenate([grad[:, 8:], new[:, 8:]], axis=1)
        send_near[after] = jnp.where(even, high, low).astype(BF16)
        send_far[after] = jnp.where(even, low, high).astype(BF16)


def one_hot(slot, offsets, sources):
    shape = (64, 64 * sources)
    lane = lax.broadcasted_iota(jnp.int32, shape, 1) - 16 * (lax.broadcasted_iota(jnp.int32, shape, 0) >> 4)
    columns = jnp.concatenate([slot[:, o : o + 1] for o in offsets], axis=0)
    return jnp.where(lane == columns, 1.0, 0.0).astype(BF16)


def widened(out, kernel_of):
    for k in range(9):
        blocks = [kernel_of(3 * k + i) for i in range(3)]
        zero = jnp.zeros_like(blocks[0])
        for j in range(4):
            row = slice(128 * (4 * k + j), 128 * (4 * k + j + 1))
            out[row, :128] = blocks[j] if j < 3 else zero
            out[row, 128:] = blocks[j - 1] if j > 0 else zero


def decoded(tile, first):
    code = tile.astype(F32)[:, :27].astype(jnp.int32)
    return code - 8 + first, code > 0


def tables_kernel(own, weight_hbm, gather_new, gather_back, wide, flipped, weight, sems):
    even = is_even()
    (copy,) = fetch((weight_hbm,), (weight,), sems)
    named, present = decoded(own[LINKS], lax.broadcasted_iota(jnp.int32, (16, 27), 0))
    outside = (named < 0) | (named >= 16)
    near_side = (named >= 8) == even
    row = named & 7
    slot = jnp.where(outside, row + jnp.where(near_side, 72, 136), named)
    slot = jnp.where(present, slot, -1024)
    for number, offsets in enumerate(MATRICES[:-1]):
        gather_new[number] = one_hot(slot, offsets, 3)
    slot = row + jnp.where(outside, 8, 0) + jnp.where(near_side, 0, 64)
    slot = jnp.where(present, slot, -1024)
    for number, offsets in enumerate(MATRICES):
        gather_back[number] = one_hot(slot, offsets, 2)
    copy.wait()
    widened(wide, lambda o: weight[o])
    widened(flipped, lambda o: weight[26 - o].T)


def fill(padded, sources, gather, count):
    for number, groups in enumerate(PLAN[:count]):
        matrix = gather(number)
        for start in range(0, len(groups), 4):
            chosen = groups[start : start + 4]
            columns = [
                jnp.concatenate([rows(u) for rows in sources for _, u in cells], axis=0) for cells in chosen
            ]
            picked = jnp.dot(
                matrix, jnp.concatenate(columns, axis=1), preferred_element_type=F32
            ).astype(BF16)
            for i, cells in enumerate(chosen):
                part = picked[:, 128 * i : 128 * i + 128].reshape(4, 16, 128)
                for j, (place, _) in enumerate(cells):
                    padded[place] = part[j]


def convolve(padded, weight, x):
    windows = []
    for dx in range(3):
        for dy in range(3):
            for j in range(4):
                windows.append(padded[x + dx : x + dx + 2, dy : dy + 4, j : j + 3 : 2].reshape(256, 128))
    both = jnp.dot(jnp.concatenate(windows, axis=1), weight[...], preferred_element_type=F32)
    halves = [both[:, 128 * h : 128 * h + 128].reshape(16, 1, 16, 128) for h in range(2)]
    return jnp.concatenate(halves, axis=1).reshape(32, 16, 128)


def sigmoid(v):
    return 1.0 / (1.0 + jnp.exp(-v))


def old_kernel(far, own, other, own_grad, wide, grad, padded):
    even = is_even()
    high = even != far
    row = lax.broadcasted_iota(jnp.int32, (16, 27), 0)
    own_named, own_present = decoded(own[LINKS], row)
    near_named, near_present = decoded(other[LINKS], row + jnp.where(high, 16, -16))

    def sides(mine, theirs):
        return jnp.concatenate(
            [jnp.where(high, mine[8:], mine[:8]), jnp.where(high, theirs[:8], theirs[8:])], axis=0
        )

    own_named = jnp.where(own_present, own_named, -1024)
    near_named = jnp.where(near_present, near_named, -1024)
    named = sides(own_named, near_named)
    slot = jnp.where((named >= 0) & (named < 16), named, (named & 15) + 64)
    slot = jnp.where(named == -1024, -1024, slot)
    fill(
        padded,
        (lambda u: own[u], lambda u: other[u]),
        lambda number: one_hot(slot, MATRICES[number], 2),
        COUNT,
    )
    for pair in range(2):
        v = convolve(padded, wide, 2 * pair)
        q = sigmoid(v)
        slope = q * (1.0 + v * (1.0 - q))
        part = slice(32 * pair, 32 * pair + 32)
        mine = own_grad[part].astype(F32)
        theirs = other[64 + 32 * pair : 96 + 32 * pair].astype(F32)
        masked = jnp.concatenate([jnp.where(high, mine[:, 8:], mine[:, :8]), theirs[:, :8]], axis=1)
        grad[part] = (masked * slope).astype(BF16)


def old_near_kernel(own, near, own_grad, wide, grad, padded):
    old_kernel(False, own, near.at[1 - (lax.axis_index("space") & 1)], own_grad, wide, grad, padded)


def old_far_kernel(own, far, own_grad, wide, grad, padded):
    old_kernel(True, own, far, own_grad, wide, grad, padded)


def store_bricks(out, pair, value, mask):
    part = slice(32 * pair, 32 * pair + 32)
    out[:, part] = jnp.swapaxes(value * mask[part].astype(F32), 0, 1).astype(BF16)


def new_kernel(own, near, far, mask, gather, wide, out, padded):
    near = near.at[1 - (lax.axis_index("space") & 1)]
    for x in range(4):
        for y in range(4):
            u = 16 * x + 4 * y
            padded[x + 1, y + 1, 1:5] = own[u : u + 4]
    fill(
        padded,
        (lambda u: own[u], lambda u: near[64 + u], lambda u: far[64 + u]),
        lambda number: gather[number],
        COUNT - 1,
    )
    for pair in range(2):
        v = convolve(padded, wide, 2 * pair)
        base = own[32 * pair : 32 * pair + 32].astype(F32)
        store_bricks(out, pair, base + v * sigmoid(v), mask)


def back_kernel(near, far, own_grad, mask, gather, flipped, out, padded):
    fill(padded, (lambda u: near[u], lambda u: far[u]), lambda number: gather[number], COUNT)
    for pair in range(2):
        v = convolve(padded, flipped, 2 * pair)
        base = own_grad[32 * pair : 32 * pair + 32].astype(F32)
        store_bricks(out, pair, base + v, mask)


PADDED = pltpu.VMEM((6, 6, 6, 16, 128), BF16)
BRICKS = pltpu.VMEM((16, 64, 128), BF16)
OCC = pltpu.VMEM((16, 64), jnp.int32)
HBM = pl.BlockSpec(memory_space=pltpu.HBM)
VMEM = pl.BlockSpec(memory_space=pltpu.VMEM)


def call(kernel, shapes, ins, out, scratch=(), flops=0):
    place = pltpu.HBM if out is HBM else pltpu.VMEM
    run = pl.pallas_call(
        kernel,
        out_shape=[place(s, BF16) for s in shapes],
        in_specs=ins,
        out_specs=[out] * len(shapes),
        scratch_shapes=list(scratch),
        compiler_params=pltpu.CompilerParams(vmem_limit_bytes=VMEM_LIMIT),
        cost_estimate=pl.CostEstimate(flops=flops, bytes_accessed=2 << 20, transcendentals=0),
    )

    def placed(*arrays):
        spaces = [pltpu.HBM if spec is HBM else pltpu.VMEM for spec in ins]
        return run(*[pltpu.with_memory_space_constraint(a, m) for a, m in zip(arrays, spaces)])

    return placed


def across(value, count):
    pairs = [(i, i + 1) for i in range(1, count - 1, 2)]
    return lax.ppermute(value, "space", pairs + [(b, a) for a, b in pairs])


def inside(value, count):
    return lax.all_gather(value, "space", axis_index_groups=[[i, i + 1] for i in range(0, count, 2)])


def flush_kernel(source, out, sem):
    copy = pltpu.make_async_copy(source, out, sem)
    copy.start()
    copy.wait()


def per_device(count, sections, incoming, saved, cotangent, occupancy, neighbours, conv_weight):
    tile = (64, 16, 128)
    payload = (LINKS + 1, 16, 128)
    send_near, send_far, own_new, own_grad, mask = call(
        prepare_kernel,
        [payload, payload, tile, tile, tile],
        [HBM] * 5,
        VMEM,
        [
            pltpu.VMEM((16, 64), jnp.int32),
            pltpu.VMEM((16, 27), jnp.int32),
            BRICKS,
            BRICKS,
            BRICKS,
            pltpu.SemaphoreType.DMA((5,)),
        ],
    )(saved[0], cotangent[0], incoming[0], occupancy[0], neighbours[0])
    far = across(send_far, count)
    gather_new, gather_back, wide, flipped = call(
        tables_kernel,
        [(COUNT - 1, 64, 192), (COUNT, 64, 128), (36 * 128, 256), (36 * 128, 256)],
        [VMEM, HBM],
        VMEM,
        [pltpu.VMEM((27, 128, 128), BF16), pltpu.SemaphoreType.DMA((1,))],
        flops=1 << 31,
    )(send_near, conv_weight[0])
    send_near, wide = lax.optimization_barrier((send_near, wide))
    near = inside(send_near, count)
    (grad_near,) = call(old_near_kernel, [tile], [VMEM] * 4, VMEM, [PADDED], flops=1 << 30)(
        send_near, near, own_grad, wide
    )
    (out,) = call(new_kernel, [(16, 64, 128)], [VMEM] * 6, VMEM, [PADDED], flops=1 << 30)(
        own_new, near, far, mask, gather_new, wide
    )
    arrived = lax.ppermute(out[None], "segment", [(s, s + 1) for s in range(sections - 1)])
    (grad_far,) = call(old_far_kernel, [tile], [VMEM] * 4, VMEM, [PADDED], flops=1 << 30)(
        send_near, far, own_grad, wide
    )
    (back,) = call(back_kernel, [(16, 64, 128)], [VMEM] * 6, VMEM, [PADDED], flops=1 << 30)(
        grad_near, grad_far, own_grad, mask, gather_back, flipped
    )
    returned = lax.ppermute(back[None], "segment", [(s + 1, s) for s in range(sections - 1)])
    (arrived,) = call(flush_kernel, [(1, 16, 64, 128)], [VMEM], HBM, [pltpu.SemaphoreType.DMA])(arrived)
    return arrived, returned


def solution(mesh):
    brick = P("segment", "space", None, None)
    index = P("segment", "space", None)
    return jax.shard_map(
        functools.partial(per_device, mesh.shape["space"], mesh.shape["segment"]),
        mesh=mesh,
        in_specs=(brick, brick, brick, index, index, P("segment", None, None, None)),
        out_specs=(brick, brick),
        check_vma=False,
    )
```

time: 43 us -> 73.2 us (1.70)
  the two profiles are of different devices: /device:TPU:198 before, /device:TPU:192 now
where the time goes in v2:
time: 73.2 us; the launch traced here: 72.8 us
  waiting for transfers between devices  28.1 us (38%)
  Pallas kernels  15.9 us (22%)
  between operations  14.2 us (19%)
  starting transfers between devices  7.42 us (10%)
  local copies, waits for them, and re-layouts  7.11 us (10%)
    all_gather x1, waiting for transfers between devices, inside(): lax.all_gather(value, 'space', axis_index_groups=[[i, i + 1] for i in ran...  19.4 us
    pallas_call x7, Pallas kernels, placed(): run(*[pltpu.with_memory_space_constraint(a, m) for a, m in zip(arrays, sp...  15.9 us
    unnamed x27, local copies, waits for them, and re-layouts  7.11 us
    ppermute x1, waiting for transfers between devices, per_device(): lax.ppermute(back[None], 'segment', [(s + 1, s) for s in range(sections -...  6.46 us
    ppermute x1, starting transfers between devices, per_device(): lax.ppermute(out[None], 'segment', [(s, s + 1) for s in range(sections -...  4.76 us
    ppermute x1, waiting for transfers between devices, per_device(): lax.ppermute(out[None], 'segment', [(s, s + 1) for s in range(sections -...  2.23 us
    ppermute x1, starting transfers between devices, per_device(): lax.ppermute(back[None], 'segment', [(s + 1, s) for s in range(sections -...  1.92 us
  transfers between devices with their start and end apart: 4, of which 3 were waited for; matrix products, arithmetic and copies ran while one was open for 0% of the time, Pallas kernels for 8%

profile of v2, /device:TPU:192, one launch (start us, length us, event | category | flops | bytes accessed | tf_op | source)
XLA Modules:
  0.0 72.8 jit_solution(10028170298319467323)
XLA Ops:
  7.2 0.0 all-gather.3.cloned.1.call-start
  7.2 2.4 %shard_map.77 = (bf16[129,16,128]{2,1,0:T(8,128)(2,1)}, bf16[129,16,128]{2,1,0:T(8,128)(2,1)S(1)}, bf16[64,16,128]{2,1,0:T(8,128)(2,1)S(1)}, bf16[64,16,128]{2,1,0:T(8,128)(2,1)S(1)}, bf16[64,16,128]{2,1,0:T(8,128)(2,1)S(1)}) custom-call(bf16[16,64,128]{2,1,0:T(8,128)(2,1)} %bitcast.13, bf16[16,64,128]{2,1,0:T(8,128)(2,1)} %bitcast.14, ...), custom_call_target="tpu_custom_call" | custom-call | bytes 2097152 | tf_op jit(solution)/shard_map/pallas_call | solution.py:292
  9.7 0.0 copy-start.8
  9.7 0.7 copy-done.8
  10.4 0.0 copy-start.12
  10.4 0.8 %copy-done.12 = bf16[129,16,128]{2,1,0:T(8,128)(2,1)} copy-done((bf16[129,16,128]{2,1,0:T(8,128)(2,1)}, bf16[129,16,128]{2,1,0:T(8,128)(2,1)S(1)}, u32[]{:S(2)}) %copy-start.12) | copy-done | bytes 528408
  11.2 2.9 %shard_map.78 = (bf16[20,64,192]{2,1,0:T(8,128)(2,1)S(1)}, bf16[21,64,128]{2,1,0:T(8,128)(2,1)S(1)}, bf16[4608,256]{1,0:T(8,128)(2,1)S(1)}, bf16[4608,256]{1,0:T(8,128)(2,1)S(1)}) custom-call(bf16[129,16,128]{2,1,0:T(8,128)(2,1)} %get-tuple-element.16.own, bf16[27,128,128]{2,1,0:T(8,128)(2,1)} %bitcast.18), custom_call_target="tpu_custom_call" | custom-call | flops 2147483648 | bytes 2097152 | tf_op jit(solution)/shard_map/pallas_call | solution.py:292
  14.0 0.0 copy-start.2
  14.1 1.4 %copy-done.2 = bf16[4608,256]{1,0:T(8,128)(2,1)} copy-done((bf16[4608,256]{1,0:T(8,128)(2,1)}, bf16[4608,256]{1,0:T(8,128)(2,1)S(1)}, u32[]{:S(2)}) %copy-start.2) | copy-done | bytes 2359320
  15.5 0.0 copy-start.6
  15.5 0.7 %copy-done.6 = bf16[21,64,128]{2,1,0:T(8,128)(2,1)} copy-done((bf16[21,64,128]{2,1,0:T(8,128)(2,1)}, bf16[21,64,128]{2,1,0:T(8,128)(2,1)S(1)}, u32[]{:S(2)}) %copy-start.6) | copy-done | bytes 344088
  16.2 0.0 all-gather.3.cloned.1.call-update
  16.2 0.7 collective-permute-start
  16.9 0.0 collective-permute-done.far
  16.9 3.0 %shard_map.82.far = bf16[64,16,128]{2,1,0:T(8,128)(2,1)S(1)} custom-call(bf16[129,16,128]{2,1,0:T(8,128)(2,1)} %get-tuple-element.16.own, bf16[129,16,128]{2,1,0:T(8,128)(2,1)S(1)} %collective-permute-done.far, bf16[64,16,128]{2,1,0:T(8,128)(2,1)S(1)} %get-tuple-element.21.own_grad, bf16[4608,256]{1,0:T(8,128)(2,1)S(1)} %get-tuple-element.20.wide), custom_call_target="tpu_custom_call" | custom-call | flops 1073741824 | bytes 2097152 | tf_op jit(solution)/shard_map/pallas_call | solution.py:292
  19.9 0.0 copy-start.4
  19.9 0.8 %copy-done.4 = bf16[129,16,128]{2,1,0:T(8,128)(2,1)} copy-done((bf16[129,16,128]{2,1,0:T(8,128)(2,1)}, bf16[129,16,128]{2,1,0:T(8,128)(2,1)S(1)}, u32[]{:S(2)}) %copy-start.4) | copy-done | bytes 528408
  20.7 0.0 copy-start.10
  20.7 0.7 copy-done.10
  21.4 19.4 %all-gather.3.cloned.1.call-done = bf16[258,16,128]{2,1,0:T(8,128)(2,1)} async-done(((bf16[129,16,128]{2,1,0:T(8,128)(2,1)}), bf16[258,16,128]{2,1,0:T(8,128)(2,1)}) %all-gather.3.cloned.1.call-update) | async-done | bytes 1056784 | tf_op jit(solution)/shard_map/all_gather | solution.py:303
  40.8 0.0 copy-start
  40.8 1.2 %copy-done = bf16[258,16,128]{2,1,0:T(8,128)(2,1)S(1)} copy-done((bf16[258,16,128]{2,1,0:T(8,128)(2,1)S(1)}, bf16[258,16,128]{2,1,0:T(8,128)(2,1)}, u32[]{:S(2)}) %copy-start) | copy-done | bytes 1056792
  42.1 0.0 copy-start.1
  42.1 0.0 copy-start.5
  42.1 0.0 copy-start.9
  42.1 3.1 %shard_map.81.near = bf16[64,16,128]{2,1,0:T(8,128)(2,1)S(1)} custom-call(bf16[129,16,128]{2,1,0:T(8,128)(2,1)} %get-tuple-element.16.own, bf16[2,129,16,128]{3,2,1,0:T(8,128)(2,1)S(1)} %bitcast.9, bf16[64,16,128]{2,1,0:T(8,128)(2,1)S(1)} %get-tuple-element.21.own_grad, bf16[4608,256]{1,0:T(8,128)(2,1)S(1)} %get-tuple-element.20.wide), custom_call_target="tpu_custom_call" | custom-call | flops 1073741824 | bytes 2097152 | tf_op jit(solution)/shard_map/pallas_call | solution.py:292
  45.2 0.0 copy-done.1
  45.2 0.0 copy-done.5
  45.2 0.0 copy-done.9
  45.2 0.0 copy-start.3
  45.2 0.0 copy-start.7
  45.2 0.0 copy-start.11
  45.2 2.1 %shard_map.79 = bf16[16,64,128]{2,1,0:T(8,128)(2,1)S(1)} custom-call(bf16[64,16,128]{2,1,0:T(8,128)(2,1)S(1)} %copy-done.9, bf16[2,129,16,128]{3,2,1,0:T(8,128)(2,1)S(1)} %bitcast.10, bf16[129,16,128]{2,1,0:T(8,128)(2,1)S(1)} %copy-done.5, bf16[64,16,128]{2,1,0:T(8,128)(2,1)S(1)} %get-tuple-element.18.mask, ...), custom_call_target="tpu_custom_call" | custom-call | flops 1073741824 | bytes 2097152 | tf_op jit(solution)/shard_map/pallas_call | solution.py:292
  47.3 4.8 %collective-permute-start.1 = (bf16[1,16,64,128]{3,2,1,0:T(8,128)(2,1)S(1)}, bf16[1,16,64,128]{3,2,1,0:T(8,128)(2,1)S(1)}, u32[]{:S(2)}, u32[]{:S(2)}) collective-permute-start(bf16[1,16,64,128]{3,2,1,0:T(8,128)(2,1)S(1)} %bitcast.11), channel_id=1, source_target_pairs={{0,1},{1,2},{2,3},{3,4},{4,5},{5,6},{6,7},{7,8},{8,9},{9,10},{10,1... | collective-permute-start | bytes 786440 | tf_op jit(solution)/shard_map/ppermute | solution.py:346
  52.1 0.0 copy-done.3
  52.1 0.0 copy-done.7
  52.1 0.0 copy-done.11
  52.1 1.8 %shard_map.83 = bf16[16,64,128]{2,1,0:T(8,128)(2,1)S(1)} custom-call(bf16[64,16,128]{2,1,0:T(8,128)(2,1)S(1)} %shard_map.81.near, bf16[64,16,128]{2,1,0:T(8,128)(2,1)S(1)} %copy-done.11, bf16[64,16,128]{2,1,0:T(8,128)(2,1)S(1)} %get-tuple-element.21.own_grad, bf16[64,16,128]{2,1,0:T(8,128)(2,1)S(1)} %get-tuple-element.18.mask, ...), custom_call_target="tpu_custom_call" | custom-call | flops 1073741824 | bytes 2097152 | tf_op jit(solution)/shard_map/pallas_call | solution.py:292
  53.9 1.9 %collective-permute-start.2 = (bf16[1,16,64,128]{3,2,1,0:T(8,128)(2,1)S(1)}, bf16[1,16,64,128]{3,2,1,0:T(8,128)(2,1)S(1)}, u32[]{:S(2)}, u32[]{:S(2)}) collective-permute-start(bf16[1,16,64,128]{3,2,1,0:T(8,128)(2,1)S(1)} %bitcast.12), channel_id=1, source_target_pairs={{1,0},{2,1},{3,2},{4,3},{5,4},{6,5},{7,6},{8,7},{9,8},{10,9},{11,1... | collective-permute-start | bytes 786440 | tf_op jit(solution)/shard_map/ppermute | solution.py:353
  55.9 2.2 %collective-permute-done.1.source = bf16[1,16,64,128]{3,2,1,0:T(8,128)(2,1)S(1)} collective-permute-done((bf16[1,16,64,128]{3,2,1,0:T(8,128)(2,1)S(1)}, bf16[1,16,64,128]{3,2,1,0:T(8,128)(2,1)S(1)}, u32[]{:S(2)}, u32[]{:S(2)}) %collective-permute-start.1) | collective-permute-done | bytes 262176 | tf_op jit(solution)/shard_map/ppermute | solution.py:346
  58.1 0.7 shard_map.80
  58.8 6.5 %collective-permute-done.2 = bf16[1,16,64,128]{3,2,1,0:T(8,128)(2,1)S(1)} collective-permute-done((bf16[1,16,64,128]{3,2,1,0:T(8,128)(2,1)S(1)}, bf16[1,16,64,128]{3,2,1,0:T(8,128)(2,1)S(1)}, u32[]{:S(2)}, u32[]{:S(2)}) %collective-permute-start.2) | collective-permute-done | bytes 262176 | tf_op jit(solution)/shard_map/ppermute | solution.py:353
  65.3 0.7 copy.9
Async XLA Ops:
  7.2 33.7 %all-gather.3.cloned.1.call-start = ((), (), s32[]{:S(2)}) async-start(), calls=%async_computation | async-start | bytes 1585152 | tf_op jit(solution)/shard_map/all_gather | solution.py:303
  9.7 0.7 copy-start.8
  10.4 0.8 %copy-start.12 = (bf16[129,16,128]{2,1,0:T(8,128)(2,1)}, bf16[129,16,128]{2,1,0:T(8,128)(2,1)S(1)}, u32[]{:S(2)}) copy-start(bf16[129,16,128]{2,1,0:T(8,128)(2,1)S(1)} %get-tuple-element.17) | copy-start | bytes 1585156
  14.0 1.4 %copy-start.2 = (bf16[4608,256]{1,0:T(8,128)(2,1)}, bf16[4608,256]{1,0:T(8,128)(2,1)S(1)}, u32[]{:S(2)}) copy-start(bf16[4608,256]{1,0:T(8,128)(2,1)S(1)} %get-tuple-element.23.flipped) | copy-start | bytes 7077892
  15.5 0.7 %copy-start.6 = (bf16[21,64,128]{2,1,0:T(8,128)(2,1)}, bf16[21,64,128]{2,1,0:T(8,128)(2,1)S(1)}, u32[]{:S(2)}) copy-start(bf16[21,64,128]{2,1,0:T(8,128)(2,1)S(1)} %get-tuple-element.22.gather) | copy-start | bytes 1032196
  16.2 0.7 collective-permute-start
  19.9 0.8 %copy-start.4 = (bf16[129,16,128]{2,1,0:T(8,128)(2,1)}, bf16[129,16,128]{2,1,0:T(8,128)(2,1)S(1)}, u32[]{:S(2)}) copy-start(bf16[129,16,128]{2,1,0:T(8,128)(2,1)S(1)} %collective-permute-done.far) | copy-start | bytes 1585156
  20.7 0.7 copy-start.10
  40.8 1.2 %copy-start = (bf16[258,16,128]{2,1,0:T(8,128)(2,1)S(1)}, bf16[258,16,128]{2,1,0:T(8,128)(2,1)}, u32[]{:S(2)}) copy-start(bf16[258,16,128]{2,1,0:T(8,128)(2,1)} %all-gather.3.cloned.1.call-done) | copy-start | bytes 3170308
  42.1 3.1 %copy-start.1 = (bf16[258,16,128]{2,1,0:T(8,128)(2,1)S(1)}, bf16[258,16,128]{2,1,0:T(8,128)(2,1)}, u32[]{:S(2)}) copy-start(bf16[258,16,128]{2,1,0:T(8,128)(2,1)} %all-gather.3.cloned.1.call-done) | copy-start | bytes 3170308
  42.1 3.1 %copy-start.5 = (bf16[129,16,128]{2,1,0:T(8,128)(2,1)S(1)}, bf16[129,16,128]{2,1,0:T(8,128)(2,1)}, u32[]{:S(2)}) copy-start(bf16[129,16,128]{2,1,0:T(8,128)(2,1)} %copy-done.4) | copy-start | bytes 1585156
  42.1 3.1 %copy-start.9 = (bf16[64,16,128]{2,1,0:T(8,128)(2,1)S(1)}, bf16[64,16,128]{2,1,0:T(8,128)(2,1)}, u32[]{:S(2)}) copy-start(bf16[64,16,128]{2,1,0:T(8,128)(2,1)} %copy-done.8) | copy-start | bytes 786436
  45.2 6.9 %copy-start.3 = (bf16[4608,256]{1,0:T(8,128)(2,1)S(1)}, bf16[4608,256]{1,0:T(8,128)(2,1)}, u32[]{:S(2)}) copy-start(bf16[4608,256]{1,0:T(8,128)(2,1)} %copy-done.2) | copy-start | bytes 7077892
  45.2 6.9 %copy-start.7 = (bf16[21,64,128]{2,1,0:T(8,128)(2,1)S(1)}, bf16[21,64,128]{2,1,0:T(8,128)(2,1)}, u32[]{:S(2)}) copy-start(bf16[21,64,128]{2,1,0:T(8,128)(2,1)} %copy-done.6) | copy-start | bytes 1032196
  45.2 6.9 %copy-start.11 = (bf16[64,16,128]{2,1,0:T(8,128)(2,1)S(1)}, bf16[64,16,128]{2,1,0:T(8,128)(2,1)}, u32[]{:S(2)}) copy-start(bf16[64,16,128]{2,1,0:T(8,128)(2,1)} %copy-done.10) | copy-start | bytes 786436
  47.3 10.8 %collective-permute-start.1 = (bf16[1,16,64,128]{3,2,1,0:T(8,128)(2,1)S(1)}, bf16[1,16,64,128]{3,2,1,0:T(8,128)(2,1)S(1)}, u32[]{:S(2)}, u32[]{:S(2)}) collective-permute-start(bf16[1,16,64,128]{3,2,1,0:T(8,128)(2,1)S(1)} %bitcast.11), channel_id=1, source_target_pairs={{0,1},{1,2},{2,3},{3,4},{4,5},{5,6},{6,7},{7,8},{8,9},{9,10},{10,1... | collective-permute-start | bytes 786440 | tf_op jit(solution)/shard_map/ppermute | solution.py:346
  53.9 11.3 %collective-permute-start.2 = (bf16[1,16,64,128]{3,2,1,0:T(8,128)(2,1)S(1)}, bf16[1,16,64,128]{3,2,1,0:T(8,128)(2,1)S(1)}, u32[]{:S(2)}, u32[]{:S(2)}) collective-permute-start(bf16[1,16,64,128]{3,2,1,0:T(8,128)(2,1)S(1)} %bitcast.12), channel_id=1, source_target_pairs={{1,0},{2,1},{3,2},{4,3},{5,4},{6,5},{7,6},{8,7},{9,8},{10,9},{11,1... | collective-permute-start | bytes 786440 | tf_op jit(solution)/shard_map/ppermute | solution.py:353
Sparse Core Ops, SparseCore 0:
  16.3 24.4 all-gather.2

commit v3 on v2

--- a/solution.py
+++ b/solution.py
@@ -64,7 +64,8 @@
 
 MATRICES, PLAN = gather_plan()
 COUNT = len(MATRICES)
-LINKS = 128
+TAIL = 62
+LINKS = 64 + TAIL
 
 
 def fetch(sources, targets, sems):
@@ -81,6 +82,31 @@
 def voxel_major(ref, mask, block):
     part = slice(16 * block, 16 * block + 16)
     return jnp.swapaxes(ref[:, part, :].astype(F32), 0, 1) * mask[part].astype(F32)
+
+
+def rows8():
+    return lax.broadcasted_iota(jnp.int32, (8, 128), 0)
+
+
+def stored_tail(rows, tail):
+    packed = []
+    for t in range(14):
+        row = t % 7 + 1
+        packed.append(jnp.where(rows8() == 0, pltpu.roll(tail[t // 7], 8 - row, 0), rows[t])[None])
+    return jnp.concatenate(packed + [rows[14:]], axis=0)
+
+
+def read_tail(payload):
+    tiles = []
+    for which in range(2):
+        parts = [jnp.zeros((8, 128), F32)] * 2
+        for row in range(1, 8):
+            tile = payload[64 + 7 * which + row - 1].astype(F32)
+            parts = [
+                jnp.where(rows8() == row, pltpu.roll(tile[8 * h : 8 * h + 8], row, 0), parts[h]) for h in range(2)
+            ]
+        tiles.append(jnp.concatenate(parts, axis=0))
+    return tiles
 
 
 def prepare_kernel(
@@ -105,9 +131,9 @@
     send_far[LINKS] = code
     for copy in copies[2:]:
         copy.wait()
-    for block in range(4):
+    tails = {}
+    for block in (3, 1, 2, 0):
         part = slice(16 * block, 16 * block + 16)
-        after = slice(64 + 16 * block, 64 + 16 * block + 16)
         old = voxel_major(saved, mask, block).astype(BF16)
         send_near[part] = old
         send_far[part] = old
@@ -115,10 +141,17 @@
         new = voxel_major(incoming, mask, block)
         own_grad[part] = grad.astype(BF16)
         own_new[part] = new.astype(BF16)
-        low = jnp.concatenate([grad[:, :8], new[:, :8]], axis=1)
-        high = jnp.concatenate([grad[:, 8:], new[:, 8:]], axis=1)
-        send_near[after] = jnp.where(even, high, low).astype(BF16)
-        send_far[after] = jnp.where(even, low, high).astype(BF16)
+        low = [pltpu.roll(v[:, :8], 1, 1) for v in (grad, new)]
+        high = [v[:, 8:] for v in (grad, new)]
+        for side, send in enumerate((send_near, send_far)):
+            rows = [jnp.where(even == (side == 0), h, l) for h, l in zip(high, low)]
+            if block == 3:
+                tails[side] = [(r[14], r[15]) for r in rows]
+                rows = [r[:14] for r in rows]
+            if block == 0:
+                rows = [stored_tail(r, tail) for r, tail in zip(rows, tails[side])]
+            size = rows[0].shape[0]
+            send[64 + 16 * block : 64 + 16 * block + size] = jnp.concatenate(rows, axis=1).astype(BF16)
 
 
 def one_hot(slot, offsets, sources):
@@ -138,18 +171,19 @@
             out[row, 128:] = blocks[j - 1] if j > 0 else zero
 
 
-def decoded(tile, first):
-    code = tile.astype(F32)[:, :27].astype(jnp.int32)
-    return code - 8 + first, code > 0
+def decoded(code, first):
+    code = code[:, :27].astype(jnp.int32)
+    return jnp.where(code > 0, code - 8 + first, -1024)
 
 
 def tables_kernel(own, weight_hbm, gather_new, gather_back, wide, flipped, weight, sems):
     even = is_even()
     (copy,) = fetch((weight_hbm,), (weight,), sems)
-    named, present = decoded(own[LINKS], lax.broadcasted_iota(jnp.int32, (16, 27), 0))
+    named = decoded(own[LINKS].astype(F32), lax.broadcasted_iota(jnp.int32, (16, 27), 0))
+    present = named > -1024
     outside = (named < 0) | (named >= 16)
     near_side = (named >= 8) == even
-    row = named & 7
+    row = (named & 7) + jnp.where(named >= 16, 1, 0)
     slot = jnp.where(outside, row + jnp.where(near_side, 72, 136), named)
     slot = jnp.where(present, slot, -1024)
     for number, offsets in enumerate(MATRICES[:-1]):
@@ -198,20 +232,17 @@
 def old_kernel(far, own, other, own_grad, wide, grad, padded):
     even = is_even()
     high = even != far
-    row = lax.broadcasted_iota(jnp.int32, (16, 27), 0)
-    own_named, own_present = decoded(own[LINKS], row)
-    near_named, near_present = decoded(other[LINKS], row + jnp.where(high, 16, -16))
-
-    def sides(mine, theirs):
-        return jnp.concatenate(
-            [jnp.where(high, mine[8:], mine[:8]), jnp.where(high, theirs[:8], theirs[8:])], axis=0
-        )
-
-    own_named = jnp.where(own_present, own_named, -1024)
-    near_named = jnp.where(near_present, near_named, -1024)
-    named = sides(own_named, near_named)
+    row = lax.broadcasted_iota(jnp.int32, (8, 27), 0)
+    mine = own[LINKS].astype(F32)
+    theirs = other[LINKS].astype(F32)
+    mine = jnp.where(high, mine[8:], mine[:8])
+    theirs = jnp.where(high, pltpu.roll(theirs[:8], 1, 0), theirs[8:])
+    mine = decoded(mine, jnp.where(high, row + 8, row))
+    theirs = decoded(theirs, jnp.where(high, 16 + ((row + 7) & 7), row - 8))
+    named = jnp.concatenate([mine, theirs], axis=0)
     slot = jnp.where((named >= 0) & (named < 16), named, (named & 15) + 64)
     slot = jnp.where(named == -1024, -1024, slot)
+    tail = [tile[None, :8] for tile in read_tail(other)]
     fill(
         padded,
         (lambda u: own[u], lambda u: other[u]),
@@ -224,8 +255,10 @@
         slope = q * (1.0 + v * (1.0 - q))
         part = slice(32 * pair, 32 * pair + 32)
         mine = own_grad[part].astype(F32)
-        theirs = other[64 + 32 * pair : 96 + 32 * pair].astype(F32)
-        masked = jnp.concatenate([jnp.where(high, mine[:, 8:], mine[:, :8]), theirs[:, :8]], axis=1)
+        theirs = other[64 + 32 * pair : min(96 + 32 * pair, LINKS)].astype(F32)[:, :8]
+        if pair == 1:
+            theirs = jnp.concatenate([theirs] + tail, axis=0)
+        masked = jnp.concatenate([jnp.where(high, mine[:, 8:], mine[:, :8]), theirs], axis=1)
         grad[part] = (masked * slope).astype(BF16)
 
 
@@ -248,9 +281,14 @@
         for y in range(4):
             u = 16 * x + 4 * y
             padded[x + 1, y + 1, 1:5] = own[u : u + 4]
+    tails = [[tile.astype(BF16) for tile in read_tail(payload)] for payload in (near, far)]
+
+    def outer(payload, which, u):
+        return payload[64 + u] if u < TAIL else tails[which][u - TAIL]
+
     fill(
         padded,
-        (lambda u: own[u], lambda u: near[64 + u], lambda u: far[64 + u]),
+        (lambda u: own[u], lambda u: outer(near, 0, u), lambda u: outer(far, 1, u)),
         lambda number: gather[number],
         COUNT - 1,
     )

time: 73.2 us -> 37.4 us (0.51)
  the two profiles are of different devices: /device:TPU:192 before, /device:TPU:253 now
where the time goes in v3:
time: 37.4 us; the launch traced here: 37.2 us
  Pallas kernels  12.1 us (32%)
  waiting for transfers between devices  11 us (29%)
  starting transfers between devices  9.72 us (26%)
  blocking collectives  2.96 us (8%)
  between operations  0.71 us (2%)
  local copies, waits for them, and re-layouts  0.7 us (2%)
    pallas_call x7, Pallas kernels, placed(): run(*[pltpu.with_memory_space_constraint(a, m) for a, m in zip(arrays, sp...  12.1 us
    ppermute x1, waiting for transfers between devices, per_device(): lax.ppermute(back[None], 'segment', [(s + 1, s) for s in range(sections -...  7.79 us
    ppermute x1, starting transfers between devices, per_device(): lax.ppermute(out[None], 'segment', [(s, s + 1) for s in range(sections -...  5.21 us
    ppermute x1, waiting for transfers between devices, across(): return lax.ppermute(value, 'space', pairs + [(b, a) for a, b in pairs])  3.23 us
    all_gather x1, blocking collectives, inside(): lax.all_gather(value, 'space', axis_index_groups=[[i, i + 1] for i in ran...  2.96 us
    ppermute x1, starting transfers between devices, across(): return lax.ppermute(value, 'space', pairs + [(b, a) for a, b in pairs])  2.59 us
    ppermute x1, starting transfers between devices, per_device(): lax.ppermute(back[None], 'segment', [(s + 1, s) for s in range(sections -...  1.92 us
  transfers between devices with their start and end apart: 3, of which 2 were waited for; matrix products, arithmetic and copies ran while one was open for 0% of the time, Pallas kernels for 22%

profile of v3, /device:TPU:253, one launch (start us, length us, event | category | flops | bytes accessed | tf_op | source)
XLA Modules:
  0.0 37.2 jit_solution(1705686734314229429)
XLA Ops:
  0.6 1.8 %shard_map.77 = (bf16[127,16,128]{2,1,0:T(8,128)(2,1)S(1)}, bf16[127,16,128]{2,1,0:T(8,128)(2,1)S(1)}, bf16[64,16,128]{2,1,0:T(8,128)(2,1)S(1)}, bf16[64,16,128]...) custom-call(bf16[16,64,128]{2,1,0:T(8,128)(2,1)} %bitcast.13, bf16[16,64,128]{2,1,0:T(8,128)(2,1)} %bitcast.14, ...), custom_call_target="tpu_custom_call" | custom-call | bytes 2097152 | tf_op jit(solution)/shard_map/pallas_call | solution.py:330
  2.4 2.6 %collective-permute-start = (bf16[127,16,128]{2,1,0:T(8,128)(2,1)S(1)}, bf16[127,16,128]{2,1,0:T(8,128)(2,1)S(1)}, u32[]{:S(2)}, u32[]{:S(2)}) collective-permute-start(bf16[127,16,128]{2,1,0:T(8,128)(2,1)S(1)} %get-tuple-element.17), channel_id=1, source_target_pairs={{12,24},{36,48},{60,72},{84,96},{108,120},{132,144},{156,168},{180... | collective-permute-start | bytes 1560584 | tf_op jit(solution)/shard_map/ppermute | solution.py:337
  5.0 1.8 %shard_map.78 = (bf16[20,64,192]{2,1,0:T(8,128)(2,1)S(1)}, bf16[21,64,128]{2,1,0:T(8,128)(2,1)S(1)}, bf16[4608,256]{1,0:T(8,128)(2,1)S(1)}, bf16[4608,256]{1,0:T(8,128)(2,1)S(1)}) custom-call(bf16[127,16,128]{2,1,0:T(8,128)(2,1)S(1)} %get-tuple-element.16.own, bf16[27,128,128]{2,1,0:T(8,128)(2,1)} %bitcast.18), custom_call_target="tpu_custom_call" | custom-call | flops 2147483648 | bytes 2097152 | tf_op jit(solution)/shard_map/pallas_call | solution.py:330
  6.8 3.0 %all-gather = bf16[254,16,128]{2,1,0:T(8,128)(2,1)S(1)} all-gather(bf16[127,16,128]{2,1,0:T(8,128)(2,1)S(1)} %get-tuple-element.16.own), channel_id=2, replica_groups={{0,12},{24,36},{48,60},{72,84},{96,108},{120,132},{144,156},{168,180},{..., dimensions={0}, use_global_device_ids=true | all-gather | bytes 1560576 | tf_op jit(solution)/shard_map/all_gather | solution.py:341
  9.8 1.9 %shard_map.81.near = bf16[64,16,128]{2,1,0:T(8,128)(2,1)S(1)} custom-call(bf16[127,16,128]{2,1,0:T(8,128)(2,1)S(1)} %get-tuple-element.16.own, bf16[2,127,16,128]{3,2,1,0:T(8,128)(2,1)S(1)} %bitcast.9, bf16[64,16,128]{2,1,0:T(8,128)(2,1)S(1)} %get-tuple-element.21.own_grad, bf16[4608,256]{1,0:T(8,128)(2,1)S(1)} %get-tuple-element.20.wide), custom_call_target="tpu_custom_call" | custom-call | flops 1073741824 | bytes 2097152 | tf_op jit(solution)/shard_map/pallas_call | solution.py:330
  11.7 3.2 %collective-permute-done.far = bf16[127,16,128]{2,1,0:T(8,128)(2,1)S(1)} collective-permute-done((bf16[127,16,128]{2,1,0:T(8,128)(2,1)S(1)}, bf16[127,16,128]{2,1,0:T(8,128)(2,1)S(1)}, u32[]{:S(2)}, u32[]{:S(2)}) %collective-permute-start) | collective-permute-done | bytes 520224 | tf_op jit(solution)/shard_map/ppermute | solution.py:337
  15.0 2.1 %shard_map.79 = bf16[16,64,128]{2,1,0:T(8,128)(2,1)S(1)} custom-call(bf16[64,16,128]{2,1,0:T(8,128)(2,1)S(1)} %get-tuple-element.13.own, bf16[2,127,16,128]{3,2,1,0:T(8,128)(2,1)S(1)} %bitcast.10, bf16[127,16,128]{2,1,0:T(8,128)(2,1)S(1)} %collective-permute-done.far, bf16[64,16,128]{2,1,0:T(8,128)(2,1)S(1)} %get-tuple-element.18.mask, ...), custom_call_target="tpu_custom_call" | custom-call | flops 1073741824 | bytes 2097152 | tf_op jit(solution)/shard_map/pallas_call | solution.py:330
  17.1 5.2 %collective-permute-start.1 = (bf16[1,16,64,128]{3,2,1,0:T(8,128)(2,1)S(1)}, bf16[1,16,64,128]{3,2,1,0:T(8,128)(2,1)S(1)}, u32[]{:S(2)}, u32[]{:S(2)}) collective-permute-start(bf16[1,16,64,128]{3,2,1,0:T(8,128)(2,1)S(1)} %bitcast.11), channel_id=1, source_target_pairs={{0,1},{1,2},{2,3},{3,4},{4,5},{5,6},{6,7},{7,8},{8,9},{9,10},{10,1... | collective-permute-start | bytes 786440 | tf_op jit(solution)/shard_map/ppermute | solution.py:384
  22.3 1.9 %shard_map.82.far = bf16[64,16,128]{2,1,0:T(8,128)(2,1)S(1)} custom-call(bf16[127,16,128]{2,1,0:T(8,128)(2,1)S(1)} %get-tuple-element.16.own, bf16[127,16,128]{2,1,0:T(8,128)(2,1)S(1)} %collective-permute-done.far, bf16[64,16,128]{2,1,0:T(8,128)(2,1)S(1)} %get-tuple-element.21.own_grad, bf16[4608,256]{1,0:T(8,128)(2,1)S(1)} %get-tuple-element.20.wide), custom_call_target="tpu_custom_call" | custom-call | flops 1073741824 | bytes 2097152 | tf_op jit(solution)/shard_map/pallas_call | solution.py:330
  24.2 1.8 %shard_map.83 = bf16[16,64,128]{2,1,0:T(8,128)(2,1)S(1)} custom-call(bf16[64,16,128]{2,1,0:T(8,128)(2,1)S(1)} %shard_map.81.near, bf16[64,16,128]{2,1,0:T(8,128)(2,1)S(1)} %shard_map.82.far, bf16[64,16,128]{2,1,0:T(8,128)(2,1)S(1)} %get-tuple-element.21.own_grad, bf16[64,16,128]{2,1,0:T(8,128)(2,1)S(1)} %get-tuple-element.18.mask, ...), custom_call_target="tpu_custom_call" | custom-call | flops 1073741824 | bytes 2097152 | tf_op jit(solution)/shard_map/pallas_call | solution.py:330
  26.1 1.9 %collective-permute-start.2 = (bf16[1,16,64,128]{3,2,1,0:T(8,128)(2,1)S(1)}, bf16[1,16,64,128]{3,2,1,0:T(8,128)(2,1)S(1)}, u32[]{:S(2)}, u32[]{:S(2)}) collective-permute-start(bf16[1,16,64,128]{3,2,1,0:T(8,128)(2,1)S(1)} %bitcast.12), channel_id=1, source_target_pairs={{1,0},{2,1},{3,2},{4,3},{5,4},{6,5},{7,6},{8,7},{9,8},{10,9},{11,1... | collective-permute-start | bytes 786440 | tf_op jit(solution)/shard_map/ppermute | solution.py:391
  28.0 0.0 collective-permute-done.1.source
  28.0 0.7 %shard_map.80 = bf16[1,16,64,128]{3,2,1,0:T(8,128)(2,1)} custom-call(bf16[1,16,64,128]{3,2,1,0:T(8,128)(2,1)S(1)} %collective-permute-done.1.source), custom_call_target="tpu_custom_call" | custom-call | bytes 2097152 | tf_op jit(solution)/shard_map/pallas_call | solution.py:330
  28.7 7.8 %collective-permute-done.2 = bf16[1,16,64,128]{3,2,1,0:T(8,128)(2,1)S(1)} collective-permute-done((bf16[1,16,64,128]{3,2,1,0:T(8,128)(2,1)S(1)}, bf16[1,16,64,128]{3,2,1,0:T(8,128)(2,1)S(1)}, u32[]{:S(2)}, u32[]{:S(2)}) %collective-permute-start.2) | collective-permute-done | bytes 262176 | tf_op jit(solution)/shard_map/ppermute | solution.py:391
  36.5 0.7 %copy.9 = bf16[1,16,64,128]{3,2,1,0:T(8,128)(2,1)} copy(bf16[1,16,64,128]{3,2,1,0:T(8,128)(2,1)S(1)} %collective-permute-done.2) | data formatting | bytes 524288
Async XLA Ops:
  2.4 12.6 %collective-permute-start = (bf16[127,16,128]{2,1,0:T(8,128)(2,1)S(1)}, bf16[127,16,128]{2,1,0:T(8,128)(2,1)S(1)}, u32[]{:S(2)}, u32[]{:S(2)}) collective-permute-start(bf16[127,16,128]{2,1,0:T(8,128)(2,1)S(1)} %get-tuple-element.17), channel_id=1, source_target_pairs={{12,24},{36,48},{60,72},{84,96},{108,120},{132,144},{156,168},{180... | collective-permute-start | bytes 1560584 | tf_op jit(solution)/shard_map/ppermute | solution.py:337
  17.1 10.9 %collective-permute-start.1 = (bf16[1,16,64,128]{3,2,1,0:T(8,128)(2,1)S(1)}, bf16[1,16,64,128]{3,2,1,0:T(8,128)(2,1)S(1)}, u32[]{:S(2)}, u32[]{:S(2)}) collective-permute-start(bf16[1,16,64,128]{3,2,1,0:T(8,128)(2,1)S(1)} %bitcast.11), channel_id=1, source_target_pairs={{0,1},{1,2},{2,3},{3,4},{4,5},{5,6},{6,7},{7,8},{8,9},{9,10},{10,1... | collective-permute-start | bytes 786440 | tf_op jit(solution)/shard_map/ppermute | solution.py:384
  26.1 10.4 %collective-permute-start.2 = (bf16[1,16,64,128]{3,2,1,0:T(8,128)(2,1)S(1)}, bf16[1,16,64,128]{3,2,1,0:T(8,128)(2,1)S(1)}, u32[]{:S(2)}, u32[]{:S(2)}) collective-permute-start(bf16[1,16,64,128]{3,2,1,0:T(8,128)(2,1)S(1)} %bitcast.12), channel_id=1, source_target_pairs={{1,0},{2,1},{3,2},{4,3},{5,4},{6,5},{7,6},{8,7},{9,8},{10,9},{11,1... | collective-permute-start | bytes 786440 | tf_op jit(solution)/shard_map/ppermute | solution.py:391

commit v4 on v3

--- a/solution.py
+++ b/solution.py
@@ -129,14 +129,17 @@
     code = jnp.concatenate([code, jnp.zeros((16, 101), F32)], axis=1).astype(BF16)
     send_near[LINKS] = code
     send_far[LINKS] = code
-    for copy in copies[2:]:
-        copy.wait()
-    tails = {}
-    for block in (3, 1, 2, 0):
+    copies[2].wait()
+    for block in range(4):
         part = slice(16 * block, 16 * block + 16)
         old = voxel_major(saved, mask, block).astype(BF16)
         send_near[part] = old
         send_far[part] = old
+    copies[3].wait()
+    copies[4].wait()
+    tails = {}
+    for block in (3, 1, 2, 0):
+        part = slice(16 * block, 16 * block + 16)
         grad = voxel_major(cotangent, mask, block)
         new = voxel_major(incoming, mask, block)
         own_grad[part] = grad.astype(BF16)
@@ -266,10 +269,6 @@
     old_kernel(False, own, near.at[1 - (lax.axis_index("space") & 1)], own_grad, wide, grad, padded)
 
 
-def old_far_kernel(own, far, own_grad, wide, grad, padded):
-    old_kernel(True, own, far, own_grad, wide, grad, padded)
-
-
 def store_bricks(out, pair, value, mask):
     part = slice(32 * pair, 32 * pair + 32)
     out[:, part] = jnp.swapaxes(value * mask[part].astype(F32), 0, 1).astype(BF16)
@@ -304,6 +303,16 @@
         v = convolve(padded, flipped, 2 * pair)
         base = own_grad[32 * pair : 32 * pair + 32].astype(F32)
         store_bricks(out, pair, base + v, mask)
+
+
+def finish_kernel(
+    own, near, far, grad_near, own_new, own_grad, mask, gather_new, gather_back, wide, flipped,
+    back, out,
+    grad_far, padded_old, padded_new, padded_back,
+):
+    old_kernel(True, own, far, own_grad, wide, grad_far, padded_old)
+    new_kernel(own_new, near, far, mask, gather_new, wide, out, padded_new)
+    back_kernel(grad_near, grad_far, own_grad, mask, gather_back, flipped, back, padded_back)
 
 
 PADDED = pltpu.VMEM((6, 6, 6, 16, 128), BF16)
@@ -378,18 +387,17 @@
     (grad_near,) = call(old_near_kernel, [tile], [VMEM] * 4, VMEM, [PADDED], flops=1 << 30)(
         send_near, near, own_grad, wide
     )
-    (out,) = call(new_kernel, [(16, 64, 128)], [VMEM] * 6, VMEM, [PADDED], flops=1 << 30)(
-        own_new, near, far, mask, gather_new, wide
-    )
+    back, out = call(
+        finish_kernel,
+        [(16, 64, 128)] * 2,
+        [VMEM] * 11,
+        VMEM,
+        [pltpu.VMEM(tile, BF16), PADDED, PADDED, PADDED],
+        flops=1 << 31,
+    )(send_near, near, far, grad_near, own_new, own_grad, mask, gather_new, gather_back, wide, flipped)
     arrived = lax.ppermute(out[None], "segment", [(s, s + 1) for s in range(sections - 1)])
-    (grad_far,) = call(old_far_kernel, [tile], [VMEM] * 4, VMEM, [PADDED], flops=1 << 30)(
-        send_near, far, own_grad, wide
-    )
-    (back,) = call(back_kernel, [(16, 64, 128)], [VMEM] * 6, VMEM, [PADDED], flops=1 << 30)(
-        grad_near, grad_far, own_grad, mask, gather_back, flipped
-    )
     returned = lax.ppermute(back[None], "segment", [(s + 1, s) for s in range(sections - 1)])
-    (arrived,) = call(flush_kernel, [(1, 16, 64, 128)], [VMEM], HBM, [pltpu.SemaphoreType.DMA])(arrived)
+    (returned,) = call(flush_kernel, [(1, 16, 64, 128)], [VMEM], HBM, [pltpu.SemaphoreType.DMA])(returned)
     return arrived, returned
 
 

time: 37.4 us -> 36.1 us (0.965)
  the two profiles are of different devices: /device:TPU:253 before, /device:TPU:64 now
where the time goes in v4:
time: 36.1 us; the launch traced here: 35.9 us
  Pallas kernels  11.4 us (32%)
  starting transfers between devices  10.7 us (30%)
  waiting for transfers between devices  7.33 us (20%)
  blocking collectives  5.08 us (14%)
  local copies, waits for them, and re-layouts  0.7 us (2%)
  between operations  0.7 us (2%)
    pallas_call x5, Pallas kernels, placed(): run(*[pltpu.with_memory_space_constraint(a, m) for a, m in zip(arrays, sp...  11.4 us
    ppermute x1, starting transfers between devices, per_device(): lax.ppermute(back[None], 'segment', [(s + 1, s) for s in range(sections -...  8.04 us
    all_gather x1, blocking collectives, inside(): lax.all_gather(value, 'space', axis_index_groups=[[i, i + 1] for i in ran...  5.08 us
    ppermute x1, waiting for transfers between devices, per_device(): lax.ppermute(back[None], 'segment', [(s + 1, s) for s in range(sections -...  3.92 us
    ppermute x1, waiting for transfers between devices, per_device(): lax.ppermute(out[None], 'segment', [(s, s + 1) for s in range(sections -...  3.4 us
    ppermute x1, starting transfers between devices, per_device(): lax.ppermute(out[None], 'segment', [(s, s + 1) for s in range(sections -...  1.92 us
  transfers between devices with their start and end apart: 3, of which 2 were waited for; matrix products, arithmetic and copies ran while one was open for 0% of the time, Pallas kernels for 12%

profile of v4, /device:TPU:64, one launch (start us, length us, event | category | flops | bytes accessed | tf_op | source)
XLA Modules:
  0.0 35.9 jit_solution(10081498018190322712)
XLA Ops:
  0.6 1.6 %shard_map.77 = (bf16[127,16,128]{2,1,0:T(8,128)(2,1)S(1)}, bf16[127,16,128]{2,1,0:T(8,128)(2,1)S(1)}, bf16[64,16,128]{2,1,0:T(8,128)(2,1)S(1)}, bf16[64,16,128]...) custom-call(bf16[16,64,128]{2,1,0:T(8,128)(2,1)} %bitcast.13, bf16[16,64,128]{2,1,0:T(8,128)(2,1)} %bitcast.14, ...), custom_call_target="tpu_custom_call" | custom-call | bytes 2097152 | tf_op jit(solution)/shard_map/pallas_call | solution.py:339
  2.3 0.7 %collective-permute-start = (bf16[127,16,128]{2,1,0:T(8,128)(2,1)S(1)}, bf16[127,16,128]{2,1,0:T(8,128)(2,1)S(1)}, u32[]{:S(2)}, u32[]{:S(2)}) collective-permute-start(bf16[127,16,128]{2,1,0:T(8,128)(2,1)S(1)} %get-tuple-element.18), channel_id=1, source_target_pairs={{12,24},{36,48},{60,72},{84,96},{108,120},{132,144},{156,168},{180... | collective-permute-start | bytes 1560584 | tf_op jit(solution)/shard_map/ppermute | solution.py:346
  3.0 1.8 %shard_map.78 = (bf16[20,64,192]{2,1,0:T(8,128)(2,1)S(1)}, bf16[21,64,128]{2,1,0:T(8,128)(2,1)S(1)}, bf16[4608,256]{1,0:T(8,128)(2,1)S(1)}, bf16[4608,256]{1,0:T(8,128)(2,1)S(1)}) custom-call(bf16[127,16,128]{2,1,0:T(8,128)(2,1)S(1)} %get-tuple-element.17.own, bf16[27,128,128]{2,1,0:T(8,128)(2,1)} %bitcast.18), custom_call_target="tpu_custom_call" | custom-call | flops 2147483648 | bytes 2097152 | tf_op jit(solution)/shard_map/pallas_call | solution.py:339
  4.8 5.1 %all-gather = bf16[254,16,128]{2,1,0:T(8,128)(2,1)S(1)} all-gather(bf16[127,16,128]{2,1,0:T(8,128)(2,1)S(1)} %get-tuple-element.17.own), channel_id=2, replica_groups={{0,12},{24,36},{48,60},{72,84},{96,108},{120,132},{144,156},{168,180},{..., dimensions={0}, use_global_device_ids=true | all-gather | bytes 1560576 | tf_op jit(solution)/shard_map/all_gather | solution.py:350
  9.9 1.9 %shard_map.79.grad_near = bf16[64,16,128]{2,1,0:T(8,128)(2,1)S(1)} custom-call(bf16[127,16,128]{2,1,0:T(8,128)(2,1)S(1)} %get-tuple-element.17.own, bf16[2,127,16,128]{3,2,1,0:T(8,128)(2,1)S(1)} %bitcast.9, bf16[64,16,128]{2,1,0:T(8,128)(2,1)S(1)} %get-tuple-element.19.own_grad, bf16[4608,256]{1,0:T(8,128)(2,1)S(1)} %get-tuple-element.20.wide), custom_call_target="tpu_custom_call" | custom-call | flops 1073741824 | bytes 2097152 | tf_op jit(solution)/shard_map/pallas_call | solution.py:339
  11.8 0.0 collective-permute-done.far
  11.8 5.3 %shard_map.80 = (bf16[16,64,128]{2,1,0:T(8,128)(2,1)S(1)}, bf16[16,64,128]{2,1,0:T(8,128)(2,1)S(1)}) custom-call(bf16[127,16,128]{2,1,0:T(8,128)(2,1)S(1)} %get-tuple-element.17.own, bf16[2,127,16,128]{3,2,1,0:T(8,128)(2,1)S(1)} %bitcast.10, bf16[127,16,128]{2,1,0:T(8,128)(2,1)S(1)} %collective-permute-done.far, ...), custom_call_target="tpu_custom_call" | custom-call | flops 2147483648 | bytes 2097152 | tf_op jit(solution)/shard_map/pallas_call | solution.py:339
  17.2 8.0 %collective-permute-start.2 = (bf16[1,16,64,128]{3,2,1,0:T(8,128)(2,1)S(1)}, bf16[1,16,64,128]{3,2,1,0:T(8,128)(2,1)S(1)}, u32[]{:S(2)}, u32[]{:S(2)}) collective-permute-start(bf16[1,16,64,128]{3,2,1,0:T(8,128)(2,1)S(1)} %bitcast.12), channel_id=1, source_target_pairs={{1,0},{2,1},{3,2},{4,3},{5,4},{6,5},{7,6},{8,7},{9,8},{10,9},{11,1... | collective-permute-start | bytes 786440 | tf_op jit(solution)/shard_map/ppermute | solution.py:399
  25.2 1.9 %collective-permute-start.1 = (bf16[1,16,64,128]{3,2,1,0:T(8,128)(2,1)S(1)}, bf16[1,16,64,128]{3,2,1,0:T(8,128)(2,1)S(1)}, u32[]{:S(2)}, u32[]{:S(2)}) collective-permute-start(bf16[1,16,64,128]{3,2,1,0:T(8,128)(2,1)S(1)} %bitcast.11), channel_id=1, source_target_pairs={{0,1},{1,2},{2,3},{3,4},{4,5},{5,6},{6,7},{7,8},{8,9},{9,10},{10,1... | collective-permute-start | bytes 786440 | tf_op jit(solution)/shard_map/ppermute | solution.py:398
  27.1 3.9 %collective-permute-done.2.source = bf16[1,16,64,128]{3,2,1,0:T(8,128)(2,1)S(1)} collective-permute-done((bf16[1,16,64,128]{3,2,1,0:T(8,128)(2,1)S(1)}, bf16[1,16,64,128]{3,2,1,0:T(8,128)(2,1)S(1)}, u32[]{:S(2)}, u32[]{:S(2)}) %collective-permute-start.2) | collective-permute-done | bytes 262176 | tf_op jit(solution)/shard_map/ppermute | solution.py:399
  31.1 0.7 %shard_map.81 = bf16[1,16,64,128]{3,2,1,0:T(8,128)(2,1)} custom-call(bf16[1,16,64,128]{3,2,1,0:T(8,128)(2,1)S(1)} %collective-permute-done.2.source), custom_call_target="tpu_custom_call" | custom-call | bytes 2097152 | tf_op jit(solution)/shard_map/pallas_call | solution.py:339
  31.8 3.4 %collective-permute-done.1 = bf16[1,16,64,128]{3,2,1,0:T(8,128)(2,1)S(1)} collective-permute-done((bf16[1,16,64,128]{3,2,1,0:T(8,128)(2,1)S(1)}, bf16[1,16,64,128]{3,2,1,0:T(8,128)(2,1)S(1)}, u32[]{:S(2)}, u32[]{:S(2)}) %collective-permute-start.1) | collective-permute-done | bytes 262176 | tf_op jit(solution)/shard_map/ppermute | solution.py:398
  35.2 0.7 %copy.9 = bf16[1,16,64,128]{3,2,1,0:T(8,128)(2,1)} copy(bf16[1,16,64,128]{3,2,1,0:T(8,128)(2,1)S(1)} %collective-permute-done.1) | data formatting | bytes 524288
Async XLA Ops:
  2.3 9.6 %collective-permute-start = (bf16[127,16,128]{2,1,0:T(8,128)(2,1)S(1)}, bf16[127,16,128]{2,1,0:T(8,128)(2,1)S(1)}, u32[]{:S(2)}, u32[]{:S(2)}) collective-permute-start(bf16[127,16,128]{2,1,0:T(8,128)(2,1)S(1)} %get-tuple-element.18), channel_id=1, source_target_pairs={{12,24},{36,48},{60,72},{84,96},{108,120},{132,144},{156,168},{180... | collective-permute-start | bytes 1560584 | tf_op jit(solution)/shard_map/ppermute | solution.py:346
  17.2 13.9 %collective-permute-start.2 = (bf16[1,16,64,128]{3,2,1,0:T(8,128)(2,1)S(1)}, bf16[1,16,64,128]{3,2,1,0:T(8,128)(2,1)S(1)}, u32[]{:S(2)}, u32[]{:S(2)}) collective-permute-start(bf16[1,16,64,128]{3,2,1,0:T(8,128)(2,1)S(1)} %bitcast.12), channel_id=1, source_target_pairs={{1,0},{2,1},{3,2},{4,3},{5,4},{6,5},{7,6},{8,7},{9,8},{10,9},{11,1... | collective-permute-start | bytes 786440 | tf_op jit(solution)/shard_map/ppermute | solution.py:399
  25.2 10.0 %collective-permute-start.1 = (bf16[1,16,64,128]{3,2,1,0:T(8,128)(2,1)S(1)}, bf16[1,16,64,128]{3,2,1,0:T(8,128)(2,1)S(1)}, u32[]{:S(2)}, u32[]{:S(2)}) collective-permute-start(bf16[1,16,64,128]{3,2,1,0:T(8,128)(2,1)S(1)} %bitcast.11), channel_id=1, source_target_pairs={{0,1},{1,2},{2,3},{3,4},{4,5},{5,6},{6,7},{7,8},{8,9},{9,10},{10,1... | collective-permute-start | bytes 786440 | tf_op jit(solution)/shard_map/ppermute | solution.py:398

commit v5 on v4

--- a/solution.py
+++ b/solution.py
@@ -110,13 +110,15 @@
 
 
 def prepare_kernel(
-    saved_hbm, cotangent_hbm, incoming_hbm, occ_hbm, links_hbm,
-    send_near, send_far, own_new, own_grad, mask,
+    saved_hbm, cotangent_hbm, incoming_hbm, occ_hbm, links_hbm, weight_hbm,
+    send_near, send_far, own_new, own_grad, mask, weight,
     occ, links, saved, cotangent, incoming, sems,
 ):
     even = is_even()
     copies = fetch(
-        (occ_hbm, links_hbm, saved_hbm, cotangent_hbm, incoming_hbm), (occ, links, saved, cotangent, incoming), sems
+        (occ_hbm, links_hbm, saved_hbm, cotangent_hbm, incoming_hbm, weight_hbm),
+        (occ, links, saved, cotangent, incoming, weight),
+        sems,
     )
     copies[0].wait()
     occupied = occ[...].astype(F32)
@@ -155,6 +157,7 @@
                 rows = [stored_tail(r, tail) for r, tail in zip(rows, tails[side])]
             size = rows[0].shape[0]
             send[64 + 16 * block : 64 + 16 * block + size] = jnp.concatenate(rows, axis=1).astype(BF16)
+    copies[5].wait()
 
 
 def one_hot(slot, offsets, sources):
@@ -179,9 +182,8 @@
     return jnp.where(code > 0, code - 8 + first, -1024)
 
 
-def tables_kernel(own, weight_hbm, gather_new, gather_back, wide, flipped, weight, sems):
+def tables_kernel(own, weight, gather_new, gather_back, wide, flipped):
     even = is_even()
-    (copy,) = fetch((weight_hbm,), (weight,), sems)
     named = decoded(own[LINKS].astype(F32), lax.broadcasted_iota(jnp.int32, (16, 27), 0))
     present = named > -1024
     outside = (named < 0) | (named >= 16)
@@ -195,7 +197,6 @@
     slot = jnp.where(present, slot, -1024)
     for number, offsets in enumerate(MATRICES):
         gather_back[number] = one_hot(slot, offsets, 2)
-    copy.wait()
     widened(wide, lambda o: weight[o])
     widened(flipped, lambda o: weight[26 - o].T)
 
@@ -359,10 +360,10 @@
 def per_device(count, sections, incoming, saved, cotangent, occupancy, neighbours, conv_weight):
     tile = (64, 16, 128)
     payload = (LINKS + 1, 16, 128)
-    send_near, send_far, own_new, own_grad, mask = call(
+    send_near, send_far, own_new, own_grad, mask, weight = call(
         prepare_kernel,
-        [payload, payload, tile, tile, tile],
-        [HBM] * 5,
+        [payload, payload, tile, tile, tile, (27, 128, 128)],
+        [HBM] * 6,
         VMEM,
         [
             pltpu.VMEM((16, 64), jnp.int32),
@@ -370,18 +371,17 @@
             BRICKS,
             BRICKS,
             BRICKS,
-            pltpu.SemaphoreType.DMA((5,)),
+            pltpu.SemaphoreType.DMA((6,)),
         ],
-    )(saved[0], cotangent[0], incoming[0], occupancy[0], neighbours[0])
+    )(saved[0], cotangent[0], incoming[0], occupancy[0], neighbours[0], conv_weight[0])
     far = across(send_far, count)
     gather_new, gather_back, wide, flipped = call(
         tables_kernel,
         [(COUNT - 1, 64, 192), (COUNT, 64, 128), (36 * 128, 256), (36 * 128, 256)],
-        [VMEM, HBM],
+        [VMEM, VMEM],
         VMEM,
-        [pltpu.VMEM((27, 128, 128), BF16), pltpu.SemaphoreType.DMA((1,))],
         flops=1 << 31,
-    )(send_near, conv_weight[0])
+    )(send_near, weight)
     send_near, wide = lax.optimization_barrier((send_near, wide))
     near = inside(send_near, count)
     (grad_near,) = call(old_near_kernel, [tile], [VMEM] * 4, VMEM, [PADDED], flops=1 << 30)(
@@ -395,8 +395,8 @@
         [pltpu.VMEM(tile, BF16), PADDED, PADDED, PADDED],
         flops=1 << 31,
     )(send_near, near, far, grad_near, own_new, own_grad, mask, gather_new, gather_back, wide, flipped)
+    returned = lax.ppermute(back[None], "segment", [(s + 1, s) for s in range(sections - 1)])
     arrived = lax.ppermute(out[None], "segment", [(s, s + 1) for s in range(sections - 1)])
-    returned = lax.ppermute(back[None], "segment", [(s + 1, s) for s in range(sections - 1)])
     (returned,) = call(flush_kernel, [(1, 16, 64, 128)], [VMEM], HBM, [pltpu.SemaphoreType.DMA])(returned)
     return arrived, returned
 

time: 36.1 us -> 35.3 us (0.978)
  Pallas kernels: 11.4 us -> 10.5 us
    pallas_call x5, Pallas kernels: 11.4 us -> 10.5 us  [placed(): run(*[pltpu.with_memory_space_constraint(a, m) for a, m in zip(arrays, sp...]
  transfers between devices with their start and end apart: 3 -> 3, of which waited for: 2 -> 2; matrix products, arithmetic and copies ran while one was open for 0% -> 0% of each run, Pallas kernels for 12% -> 10%
where the time goes in v5:
time: 35.3 us; the launch traced here: 35 us
  starting transfers between devices  10.7 us (30%)
  Pallas kernels  10.5 us (30%)
  waiting for transfers between devices  7.33 us (21%)
  blocking collectives  5.08 us (14%)
  local copies, waits for them, and re-layouts  0.7 us (2%)
  between operations  0.7 us (2%)
    pallas_call x5, Pallas kernels, placed(): run(*[pltpu.with_memory_space_constraint(a, m) for a, m in zip(arrays, sp...  10.5 us
    ppermute x1, starting transfers between devices, per_device(): lax.ppermute(back[None], 'segment', [(s + 1, s) for s in range(sections -...  8.04 us
    all_gather x1, blocking collectives, inside(): lax.all_gather(value, 'space', axis_index_groups=[[i, i + 1] for i in ran...  5.08 us
    ppermute x1, waiting for transfers between devices, per_device(): lax.ppermute(back[None], 'segment', [(s + 1, s) for s in range(sections -...  3.92 us
    ppermute x1, waiting for transfers between devices, per_device(): lax.ppermute(out[None], 'segment', [(s, s + 1) for s in range(sections -...  3.4 us
    ppermute x1, starting transfers between devices, per_device(): lax.ppermute(out[None], 'segment', [(s, s + 1) for s in range(sections -...  1.92 us
  transfers between devices with their start and end apart: 3, of which 2 were waited for; matrix products, arithmetic and copies ran while one was open for 0% of the time, Pallas kernels for 10%

profile of v5, /device:TPU:64, one launch (start us, length us, event | category | flops | bytes accessed | tf_op | source)
XLA Modules:
  0.0 35.0 jit_solution(9030549103120779493)
XLA Ops:
  0.6 1.6 %shard_map.77 = (bf16[127,16,128]{2,1,0:T(8,128)(2,1)S(1)}, bf16[127,16,128]{2,1,0:T(8,128)(2,1)S(1)}, bf16[64,16,128]{2,1,0:T(8,128)(2,1)S(1)}, bf16[64,16,128]...) custom-call(bf16[16,64,128]{2,1,0:T(8,128)(2,1)} %bitcast.14, ...), custom_call_target="tpu_custom_call" | custom-call | bytes 2097152 | tf_op jit(solution)/shard_map/pallas_call | solution.py:340
  2.3 0.7 %collective-permute-start = (bf16[127,16,128]{2,1,0:T(8,128)(2,1)S(1)}, bf16[127,16,128]{2,1,0:T(8,128)(2,1)S(1)}, u32[]{:S(2)}, u32[]{:S(2)}) collective-permute-start(bf16[127,16,128]{2,1,0:T(8,128)(2,1)S(1)} %get-tuple-element.20), channel_id=1, source_target_pairs={{12,24},{36,48},{60,72},{84,96},{108,120},{132,144},{156,168},{180... | collective-permute-start | bytes 1560584 | tf_op jit(solution)/shard_map/ppermute | solution.py:347
  3.0 1.0 %shard_map.78 = (bf16[20,64,192]{2,1,0:T(8,128)(2,1)S(1)}, bf16[21,64,128]{2,1,0:T(8,128)(2,1)S(1)}, bf16[4608,256]{1,0:T(8,128)(2,1)S(1)}, bf16[4608,256]{1,0:T(8,128)(2,1)S(1)}) custom-call(bf16[127,16,128]{2,1,0:T(8,128)(2,1)S(1)} %get-tuple-element.19.own, bf16[27,128,128]{2,1,0:T(8,128)(2,1)S(1)} %get-tuple-element.17.weight), custom_call_target="tpu_custom_call" | custom-call | flops 2147483648 | bytes 2097152 | tf_op jit(solution)/shard_map/pallas_call | solution.py:340
  3.9 5.1 %all-gather = bf16[254,16,128]{2,1,0:T(8,128)(2,1)S(1)} all-gather(bf16[127,16,128]{2,1,0:T(8,128)(2,1)S(1)} %get-tuple-element.19.own), channel_id=2, replica_groups={{0,12},{24,36},{48,60},{72,84},{96,108},{120,132},{144,156},{168,180},{..., dimensions={0}, use_global_device_ids=true | all-gather | bytes 1560576 | tf_op jit(solution)/shard_map/all_gather | solution.py:351
  9.0 1.9 %shard_map.79.grad_near = bf16[64,16,128]{2,1,0:T(8,128)(2,1)S(1)} custom-call(bf16[127,16,128]{2,1,0:T(8,128)(2,1)S(1)} %get-tuple-element.19.own, bf16[2,127,16,128]{3,2,1,0:T(8,128)(2,1)S(1)} %bitcast.9, bf16[64,16,128]{2,1,0:T(8,128)(2,1)S(1)} %get-tuple-element.21.own_grad, bf16[4608,256]{1,0:T(8,128)(2,1)S(1)} %get-tuple-element.22.wide), custom_call_target="tpu_custom_call" | custom-call | flops 1073741824 | bytes 2097152 | tf_op jit(solution)/shard_map/pallas_call | solution.py:340
  11.0 0.0 collective-permute-done.far
  11.0 5.3 %shard_map.80 = (bf16[16,64,128]{2,1,0:T(8,128)(2,1)S(1)}, bf16[16,64,128]{2,1,0:T(8,128)(2,1)S(1)}) custom-call(bf16[127,16,128]{2,1,0:T(8,128)(2,1)S(1)} %get-tuple-element.19.own, bf16[2,127,16,128]{3,2,1,0:T(8,128)(2,1)S(1)} %bitcast.10, bf16[127,16,128]{2,1,0:T(8,128)(2,1)S(1)} %collective-permute-done.far, ...), custom_call_target="tpu_custom_call" | custom-call | flops 2147483648 | bytes 2097152 | tf_op jit(solution)/shard_map/pallas_call | solution.py:340
  16.3 8.0 %collective-permute-start.2 = (bf16[1,16,64,128]{3,2,1,0:T(8,128)(2,1)S(1)}, bf16[1,16,64,128]{3,2,1,0:T(8,128)(2,1)S(1)}, u32[]{:S(2)}, u32[]{:S(2)}) collective-permute-start(bf16[1,16,64,128]{3,2,1,0:T(8,128)(2,1)S(1)} %bitcast.12), channel_id=1, source_target_pairs={{1,0},{2,1},{3,2},{4,3},{5,4},{6,5},{7,6},{8,7},{9,8},{10,9},{11,1... | collective-permute-start | bytes 786440 | tf_op jit(solution)/shard_map/ppermute | solution.py:398
  24.3 1.9 %collective-permute-start.1 = (bf16[1,16,64,128]{3,2,1,0:T(8,128)(2,1)S(1)}, bf16[1,16,64,128]{3,2,1,0:T(8,128)(2,1)S(1)}, u32[]{:S(2)}, u32[]{:S(2)}) collective-permute-start(bf16[1,16,64,128]{3,2,1,0:T(8,128)(2,1)S(1)} %bitcast.11), channel_id=1, source_target_pairs={{0,1},{1,2},{2,3},{3,4},{4,5},{5,6},{6,7},{7,8},{8,9},{9,10},{10,1... | collective-permute-start | bytes 786440 | tf_op jit(solution)/shard_map/ppermute | solution.py:399
  26.3 3.9 %collective-permute-done.2.source = bf16[1,16,64,128]{3,2,1,0:T(8,128)(2,1)S(1)} collective-permute-done((bf16[1,16,64,128]{3,2,1,0:T(8,128)(2,1)S(1)}, bf16[1,16,64,128]{3,2,1,0:T(8,128)(2,1)S(1)}, u32[]{:S(2)}, u32[]{:S(2)}) %collective-permute-start.2) | collective-permute-done | bytes 262176 | tf_op jit(solution)/shard_map/ppermute | solution.py:398
  30.2 0.7 %shard_map.81 = bf16[1,16,64,128]{3,2,1,0:T(8,128)(2,1)} custom-call(bf16[1,16,64,128]{3,2,1,0:T(8,128)(2,1)S(1)} %collective-permute-done.2.source), custom_call_target="tpu_custom_call" | custom-call | bytes 2097152 | tf_op jit(solution)/shard_map/pallas_call | solution.py:340
  30.9 3.4 %collective-permute-done.1 = bf16[1,16,64,128]{3,2,1,0:T(8,128)(2,1)S(1)} collective-permute-done((bf16[1,16,64,128]{3,2,1,0:T(8,128)(2,1)S(1)}, bf16[1,16,64,128]{3,2,1,0:T(8,128)(2,1)S(1)}, u32[]{:S(2)}, u32[]{:S(2)}) %collective-permute-start.1) | collective-permute-done | bytes 262176 | tf_op jit(solution)/shard_map/ppermute | solution.py:399
  34.3 0.7 %copy.9 = bf16[1,16,64,128]{3,2,1,0:T(8,128)(2,1)} copy(bf16[1,16,64,128]{3,2,1,0:T(8,128)(2,1)S(1)} %collective-permute-done.1) | data formatting | bytes 524288
Async XLA Ops:
  2.3 8.7 %collective-permute-start = (bf16[127,16,128]{2,1,0:T(8,128)(2,1)S(1)}, bf16[127,16,128]{2,1,0:T(8,128)(2,1)S(1)}, u32[]{:S(2)}, u32[]{:S(2)}) collective-permute-start(bf16[127,16,128]{2,1,0:T(8,128)(2,1)S(1)} %get-tuple-element.20), channel_id=1, source_target_pairs={{12,24},{36,48},{60,72},{84,96},{108,120},{132,144},{156,168},{180... | collective-permute-start | bytes 1560584 | tf_op jit(solution)/shard_map/ppermute | solution.py:347
  16.3 13.9 %collective-permute-start.2 = (bf16[1,16,64,128]{3,2,1,0:T(8,128)(2,1)S(1)}, bf16[1,16,64,128]{3,2,1,0:T(8,128)(2,1)S(1)}, u32[]{:S(2)}, u32[]{:S(2)}) collective-permute-start(bf16[1,16,64,128]{3,2,1,0:T(8,128)(2,1)S(1)} %bitcast.12), channel_id=1, source_target_pairs={{1,0},{2,1},{3,2},{4,3},{5,4},{6,5},{7,6},{8,7},{9,8},{10,9},{11,1... | collective-permute-start | bytes 786440 | tf_op jit(solution)/shard_map/ppermute | solution.py:398
  24.3 10.0 %collective-permute-start.1 = (bf16[1,16,64,128]{3,2,1,0:T(8,128)(2,1)S(1)}, bf16[1,16,64,128]{3,2,1,0:T(8,128)(2,1)S(1)}, u32[]{:S(2)}, u32[]{:S(2)}) collective-permute-start(bf16[1,16,64,128]{3,2,1,0:T(8,128)(2,1)S(1)} %bitcast.11), channel_id=1, source_target_pairs={{0,1},{1,2},{2,3},{3,4},{4,5},{5,6},{6,7},{7,8},{8,9},{9,10},{10,1... | collective-permute-start | bytes 786440 | tf_op jit(solution)/shard_map/ppermute | solution.py:399

commit v6 on v5

--- a/solution.py
+++ b/solution.py
@@ -230,7 +230,7 @@
 
 
 def sigmoid(v):
-    return 1.0 / (1.0 + jnp.exp(-v))
+    return 0.5 * jnp.tanh(0.5 * v) + 0.5
 
 
 def old_kernel(far, own, other, own_grad, wide, grad, padded):
@@ -275,7 +275,7 @@
     out[:, part] = jnp.swapaxes(value * mask[part].astype(F32), 0, 1).astype(BF16)
 
 
-def new_kernel(own, near, far, mask, gather, wide, out, padded):
+def new_fill(own, near, far, gather, padded):
     near = near.at[1 - (lax.axis_index("space") & 1)]
     for x in range(4):
         for y in range(4):
@@ -292,6 +292,9 @@
         lambda number: gather[number],
         COUNT - 1,
     )
+
+
+def new_rest(own, mask, wide, out, padded):
     for pair in range(2):
         v = convolve(padded, wide, 2 * pair)
         base = own[32 * pair : 32 * pair + 32].astype(F32)
@@ -311,8 +314,9 @@
     back, out,
     grad_far, padded_old, padded_new, padded_back,
 ):
+    new_fill(own_new, near, far, gather_new, padded_new)
     old_kernel(True, own, far, own_grad, wide, grad_far, padded_old)
-    new_kernel(own_new, near, far, mask, gather_new, wide, out, padded_new)
+    new_rest(own_new, mask, wide, out, padded_new)
     back_kernel(grad_near, grad_far, own_grad, mask, gather_back, flipped, back, padded_back)
 
 

time: 35.3 us -> 35.2 us (level)
  no operation moved by 1% of the time
where the time goes in v6:
time: 35.2 us; the launch traced here: 35 us
  starting transfers between devices  10.7 us (30%)
  Pallas kernels  10.5 us (30%)
  waiting for transfers between devices  7.31 us (21%)
  blocking collectives  5.08 us (14%)
  local copies, waits for them, and re-layouts  0.7 us (2%)
  between operations  0.7 us (2%)
    pallas_call x5, Pallas kernels, placed(): run(*[pltpu.with_memory_space_constraint(a, m) for a, m in zip(arrays, sp...  10.5 us
    ppermute x1, starting transfers between devices, per_device(): lax.ppermute(back[None], 'segment', [(s + 1, s) for s in range(sections -...  8.04 us
    all_gather x1, blocking collectives, inside(): lax.all_gather(value, 'space', axis_index_groups=[[i, i + 1] for i in ran...  5.08 us
    ppermute x1, waiting for transfers between devices, per_device(): lax.ppermute(back[None], 'segment', [(s + 1, s) for s in range(sections -...  3.91 us
    ppermute x1, waiting for transfers between devices, per_device(): lax.ppermute(out[None], 'segment', [(s, s + 1) for s in range(sections -...  3.4 us
    ppermute x1, starting transfers between devices, per_device(): lax.ppermute(out[None], 'segment', [(s, s + 1) for s in range(sections -...  1.92 us
  transfers between devices with their start and end apart: 3, of which 2 were waited for; matrix products, arithmetic and copies ran while one was open for 0% of the time, Pallas kernels for 10%

profile of v6, /device:TPU:64, one launch (start us, length us, event | category | flops | bytes accessed | tf_op | source)
XLA Modules:
  0.0 35.0 jit_solution(4303435491678252499)
XLA Ops:
  0.6 1.6 %shard_map.77 = (bf16[127,16,128]{2,1,0:T(8,128)(2,1)S(1)}, bf16[127,16,128]{2,1,0:T(8,128)(2,1)S(1)}, bf16[64,16,128]{2,1,0:T(8,128)(2,1)S(1)}, bf16[64,16,128]...) custom-call(bf16[16,64,128]{2,1,0:T(8,128)(2,1)} %bitcast.14, ...), custom_call_target="tpu_custom_call" | custom-call | bytes 2097152 | tf_op jit(solution)/shard_map/pallas_call | solution.py:344
  2.3 0.7 %collective-permute-start = (bf16[127,16,128]{2,1,0:T(8,128)(2,1)S(1)}, bf16[127,16,128]{2,1,0:T(8,128)(2,1)S(1)}, u32[]{:S(2)}, u32[]{:S(2)}) collective-permute-start(bf16[127,16,128]{2,1,0:T(8,128)(2,1)S(1)} %get-tuple-element.20), channel_id=1, source_target_pairs={{12,24},{36,48},{60,72},{84,96},{108,120},{132,144},{156,168},{180... | collective-permute-start | bytes 1560584 | tf_op jit(solution)/shard_map/ppermute | solution.py:351
  3.0 1.0 %shard_map.78 = (bf16[20,64,192]{2,1,0:T(8,128)(2,1)S(1)}, bf16[21,64,128]{2,1,0:T(8,128)(2,1)S(1)}, bf16[4608,256]{1,0:T(8,128)(2,1)S(1)}, bf16[4608,256]{1,0:T(8,128)(2,1)S(1)}) custom-call(bf16[127,16,128]{2,1,0:T(8,128)(2,1)S(1)} %get-tuple-element.19.own, bf16[27,128,128]{2,1,0:T(8,128)(2,1)S(1)} %get-tuple-element.17.weight), custom_call_target="tpu_custom_call" | custom-call | flops 2147483648 | bytes 2097152 | tf_op jit(solution)/shard_map/pallas_call | solution.py:344
  3.9 5.1 %all-gather = bf16[254,16,128]{2,1,0:T(8,128)(2,1)S(1)} all-gather(bf16[127,16,128]{2,1,0:T(8,128)(2,1)S(1)} %get-tuple-element.19.own), channel_id=2, replica_groups={{0,12},{24,36},{48,60},{72,84},{96,108},{120,132},{144,156},{168,180},{..., dimensions={0}, use_global_device_ids=true | all-gather | bytes 1560576 | tf_op jit(solution)/shard_map/all_gather | solution.py:355
  9.0 1.9 %shard_map.79.grad_near = bf16[64,16,128]{2,1,0:T(8,128)(2,1)S(1)} custom-call(bf16[127,16,128]{2,1,0:T(8,128)(2,1)S(1)} %get-tuple-element.19.own, bf16[2,127,16,128]{3,2,1,0:T(8,128)(2,1)S(1)} %bitcast.9, bf16[64,16,128]{2,1,0:T(8,128)(2,1)S(1)} %get-tuple-element.21.own_grad, bf16[4608,256]{1,0:T(8,128)(2,1)S(1)} %get-tuple-element.22.wide), custom_call_target="tpu_custom_call" | custom-call | flops 1073741824 | bytes 2097152 | tf_op jit(solution)/shard_map/pallas_call | solution.py:344
  10.9 0.0 collective-permute-done.far
  10.9 5.3 %shard_map.80 = (bf16[16,64,128]{2,1,0:T(8,128)(2,1)S(1)}, bf16[16,64,128]{2,1,0:T(8,128)(2,1)S(1)}) custom-call(bf16[127,16,128]{2,1,0:T(8,128)(2,1)S(1)} %get-tuple-element.19.own, bf16[2,127,16,128]{3,2,1,0:T(8,128)(2,1)S(1)} %bitcast.10, bf16[127,16,128]{2,1,0:T(8,128)(2,1)S(1)} %collective-permute-done.far, ...), custom_call_target="tpu_custom_call" | custom-call | flops 2147483648 | bytes 2097152 | tf_op jit(solution)/shard_map/pallas_call | solution.py:344
  16.3 8.0 %collective-permute-start.2 = (bf16[1,16,64,128]{3,2,1,0:T(8,128)(2,1)S(1)}, bf16[1,16,64,128]{3,2,1,0:T(8,128)(2,1)S(1)}, u32[]{:S(2)}, u32[]{:S(2)}) collective-permute-start(bf16[1,16,64,128]{3,2,1,0:T(8,128)(2,1)S(1)} %bitcast.12), channel_id=1, source_target_pairs={{1,0},{2,1},{3,2},{4,3},{5,4},{6,5},{7,6},{8,7},{9,8},{10,9},{11,1... | collective-permute-start | bytes 786440 | tf_op jit(solution)/shard_map/ppermute | solution.py:402
  24.3 1.9 %collective-permute-start.1 = (bf16[1,16,64,128]{3,2,1,0:T(8,128)(2,1)S(1)}, bf16[1,16,64,128]{3,2,1,0:T(8,128)(2,1)S(1)}, u32[]{:S(2)}, u32[]{:S(2)}) collective-permute-start(bf16[1,16,64,128]{3,2,1,0:T(8,128)(2,1)S(1)} %bitcast.11), channel_id=1, source_target_pairs={{0,1},{1,2},{2,3},{3,4},{4,5},{5,6},{6,7},{7,8},{8,9},{9,10},{10,1... | collective-permute-start | bytes 786440 | tf_op jit(solution)/shard_map/ppermute | solution.py:403
  26.2 3.9 %collective-permute-done.2.source = bf16[1,16,64,128]{3,2,1,0:T(8,128)(2,1)S(1)} collective-permute-done((bf16[1,16,64,128]{3,2,1,0:T(8,128)(2,1)S(1)}, bf16[1,16,64,128]{3,2,1,0:T(8,128)(2,1)S(1)}, u32[]{:S(2)}, u32[]{:S(2)}) %collective-permute-start.2) | collective-permute-done | bytes 262176 | tf_op jit(solution)/shard_map/ppermute | solution.py:402
  30.1 0.7 %shard_map.81 = bf16[1,16,64,128]{3,2,1,0:T(8,128)(2,1)} custom-call(bf16[1,16,64,128]{3,2,1,0:T(8,128)(2,1)S(1)} %collective-permute-done.2.source), custom_call_target="tpu_custom_call" | custom-call | bytes 2097152 | tf_op jit(solution)/shard_map/pallas_call | solution.py:344
  30.9 3.4 %collective-permute-done.1 = bf16[1,16,64,128]{3,2,1,0:T(8,128)(2,1)S(1)} collective-permute-done((bf16[1,16,64,128]{3,2,1,0:T(8,128)(2,1)S(1)}, bf16[1,16,64,128]{3,2,1,0:T(8,128)(2,1)S(1)}, u32[]{:S(2)}, u32[]{:S(2)}) %collective-permute-start.1) | collective-permute-done | bytes 262176 | tf_op jit(solution)/shard_map/ppermute | solution.py:403
  34.3 0.7 %copy.9 = bf16[1,16,64,128]{3,2,1,0:T(8,128)(2,1)} copy(bf16[1,16,64,128]{3,2,1,0:T(8,128)(2,1)S(1)} %collective-permute-done.1) | data formatting | bytes 524288
Async XLA Ops:
  2.3 8.7 %collective-permute-start = (bf16[127,16,128]{2,1,0:T(8,128)(2,1)S(1)}, bf16[127,16,128]{2,1,0:T(8,128)(2,1)S(1)}, u32[]{:S(2)}, u32[]{:S(2)}) collective-permute-start(bf16[127,16,128]{2,1,0:T(8,128)(2,1)S(1)} %get-tuple-element.20), channel_id=1, source_target_pairs={{12,24},{36,48},{60,72},{84,96},{108,120},{132,144},{156,168},{180... | collective-permute-start | bytes 1560584 | tf_op jit(solution)/shard_map/ppermute | solution.py:351
  16.3 13.9 %collective-permute-start.2 = (bf16[1,16,64,128]{3,2,1,0:T(8,128)(2,1)S(1)}, bf16[1,16,64,128]{3,2,1,0:T(8,128)(2,1)S(1)}, u32[]{:S(2)}, u32[]{:S(2)}) collective-permute-start(bf16[1,16,64,128]{3,2,1,0:T(8,128)(2,1)S(1)} %bitcast.12), channel_id=1, source_target_pairs={{1,0},{2,1},{3,2},{4,3},{5,4},{6,5},{7,6},{8,7},{9,8},{10,9},{11,1... | collective-permute-start | bytes 786440 | tf_op jit(solution)/shard_map/ppermute | solution.py:402
  24.3 10.0 %collective-permute-start.1 = (bf16[1,16,64,128]{3,2,1,0:T(8,128)(2,1)S(1)}, bf16[1,16,64,128]{3,2,1,0:T(8,128)(2,1)S(1)}, u32[]{:S(2)}, u32[]{:S(2)}) collective-permute-start(bf16[1,16,64,128]{3,2,1,0:T(8,128)(2,1)S(1)} %bitcast.11), channel_id=1, source_target_pairs={{0,1},{1,2},{2,3},{3,4},{4,5},{5,6},{6,7},{7,8},{8,9},{9,10},{10,1... | collective-permute-start | bytes 786440 | tf_op jit(solution)/shard_map/ppermute | solution.py:403

commit v7 on v5

--- a/solution.py
+++ b/solution.py
@@ -351,10 +351,9 @@
     return lax.all_gather(value, "space", axis_index_groups=[[i, i + 1] for i in range(0, count, 2)])
 
 
-def flush_kernel(source, out, sem):
-    copy = pltpu.make_async_copy(source, out, sem)
-    copy.start()
-    copy.wait()
+def flush_kernel(first, second, first_out, second_out, sems):
+    for copy in fetch((first, second), (first_out, second_out), sems):
+        copy.wait()
 
 
 def per_device(count, sections, incoming, saved, cotangent, occupancy, neighbours, conv_weight):
@@ -397,7 +396,9 @@
     )(send_near, near, far, grad_near, own_new, own_grad, mask, gather_new, gather_back, wide, flipped)
     returned = lax.ppermute(back[None], "segment", [(s + 1, s) for s in range(sections - 1)])
     arrived = lax.ppermute(out[None], "segment", [(s, s + 1) for s in range(sections - 1)])
-    (returned,) = call(flush_kernel, [(1, 16, 64, 128)], [VMEM], HBM, [pltpu.SemaphoreType.DMA])(returned)
+    arrived, returned = call(
+        flush_kernel, [(1, 16, 64, 128)] * 2, [VMEM] * 2, HBM, [pltpu.SemaphoreType.DMA((2,))]
+    )(arrived, returned)
     return arrived, returned
 
 

time: 35.3 us -> 35.4 us (level)
  waiting for transfers between devices: 7.33 us -> 8.04 us
  local copies, waits for them, and re-layouts: 0.7 us -> 0 us
    ppermute x1, waiting for transfers between devices: 3.4 us -> 4.12 us  [per_device(): lax.ppermute(out[None], 'segment', [(s, s + 1) for s in range(sections -...]
    unnamed x1 -> x0, local copies, waits for them, and re-layouts: 0.7 us -> none
  transfers between devices with their start and end apart: 3 -> 3, of which waited for: 2 -> 2; matrix products, arithmetic and copies ran while one was open for 0% -> 0% of each run, Pallas kernels for 10% -> 8%
where the time goes in v7:
time: 35.4 us; the launch traced here: 35.1 us
  starting transfers between devices  10.7 us (30%)
  Pallas kernels  10.6 us (30%)
  waiting for transfers between devices  8.04 us (23%)
  blocking collectives  5.08 us (14%)
  between operations  0.69 us (2%)
    pallas_call x5, Pallas kernels, placed(): run(*[pltpu.with_memory_space_constraint(a, m) for a, m in zip(arrays, sp...  10.6 us
    ppermute x1, starting transfers between devices, per_device(): lax.ppermute(back[None], 'segment', [(s + 1, s) for s in range(sections -...  8.05 us
    all_gather x1, blocking collectives, inside(): lax.all_gather(value, 'space', axis_index_groups=[[i, i + 1] for i in ran...  5.08 us
    ppermute x1, waiting for transfers between devices, per_device(): lax.ppermute(out[None], 'segment', [(s, s + 1) for s in range(sections -...  4.12 us
    ppermute x1, waiting for transfers between devices, per_device(): lax.ppermute(back[None], 'segment', [(s + 1, s) for s in range(sections -...  3.92 us
    ppermute x1, starting transfers between devices, per_device(): lax.ppermute(out[None], 'segment', [(s, s + 1) for s in range(sections -...  1.92 us
  transfers between devices with their start and end apart: 3, of which 2 were waited for; matrix products, arithmetic and copies ran while one was open for 0% of the time, Pallas kernels for 8%

profile of v7, /device:TPU:64, one launch (start us, length us, event | category | flops | bytes accessed | tf_op | source)
XLA Modules:
  0.0 35.1 jit_solution(1130085234932934147)
XLA Ops:
  0.6 1.6 %shard_map.77 = (bf16[127,16,128]{2,1,0:T(8,128)(2,1)S(1)}, bf16[127,16,128]{2,1,0:T(8,128)(2,1)S(1)}, bf16[64,16,128]{2,1,0:T(8,128)(2,1)S(1)}, bf16[64,16,128]...) custom-call(bf16[16,64,128]{2,1,0:T(8,128)(2,1)} %bitcast.14, ...), custom_call_target="tpu_custom_call" | custom-call | bytes 2097152 | tf_op jit(solution)/shard_map/pallas_call | solution.py:340
  2.3 0.7 %collective-permute-start = (bf16[127,16,128]{2,1,0:T(8,128)(2,1)S(1)}, bf16[127,16,128]{2,1,0:T(8,128)(2,1)S(1)}, u32[]{:S(2)}, u32[]{:S(2)}) collective-permute-start(bf16[127,16,128]{2,1,0:T(8,128)(2,1)S(1)} %get-tuple-element.20), channel_id=1, source_target_pairs={{12,24},{36,48},{60,72},{84,96},{108,120},{132,144},{156,168},{180... | collective-permute-start | bytes 1560584 | tf_op jit(solution)/shard_map/ppermute | solution.py:347
  3.0 1.0 %shard_map.78 = (bf16[20,64,192]{2,1,0:T(8,128)(2,1)S(1)}, bf16[21,64,128]{2,1,0:T(8,128)(2,1)S(1)}, bf16[4608,256]{1,0:T(8,128)(2,1)S(1)}, bf16[4608,256]{1,0:T(8,128)(2,1)S(1)}) custom-call(bf16[127,16,128]{2,1,0:T(8,128)(2,1)S(1)} %get-tuple-element.19.own, bf16[27,128,128]{2,1,0:T(8,128)(2,1)S(1)} %get-tuple-element.17.weight), custom_call_target="tpu_custom_call" | custom-call | flops 2147483648 | bytes 2097152 | tf_op jit(solution)/shard_map/pallas_call | solution.py:340
  3.9 5.1 %all-gather = bf16[254,16,128]{2,1,0:T(8,128)(2,1)S(1)} all-gather(bf16[127,16,128]{2,1,0:T(8,128)(2,1)S(1)} %get-tuple-element.19.own), channel_id=2, replica_groups={{0,12},{24,36},{48,60},{72,84},{96,108},{120,132},{144,156},{168,180},{..., dimensions={0}, use_global_device_ids=true | all-gather | bytes 1560576 | tf_op jit(solution)/shard_map/all_gather | solution.py:351
  9.0 1.9 %shard_map.79.grad_near = bf16[64,16,128]{2,1,0:T(8,128)(2,1)S(1)} custom-call(bf16[127,16,128]{2,1,0:T(8,128)(2,1)S(1)} %get-tuple-element.19.own, bf16[2,127,16,128]{3,2,1,0:T(8,128)(2,1)S(1)} %bitcast.9, bf16[64,16,128]{2,1,0:T(8,128)(2,1)S(1)} %get-tuple-element.21.own_grad, bf16[4608,256]{1,0:T(8,128)(2,1)S(1)} %get-tuple-element.22.wide), custom_call_target="tpu_custom_call" | custom-call | flops 1073741824 | bytes 2097152 | tf_op jit(solution)/shard_map/pallas_call | solution.py:340
  11.0 0.0 collective-permute-done.far
  11.0 5.3 %shard_map.80 = (bf16[16,64,128]{2,1,0:T(8,128)(2,1)S(1)}, bf16[16,64,128]{2,1,0:T(8,128)(2,1)S(1)}) custom-call(bf16[127,16,128]{2,1,0:T(8,128)(2,1)S(1)} %get-tuple-element.19.own, bf16[2,127,16,128]{3,2,1,0:T(8,128)(2,1)S(1)} %bitcast.10, bf16[127,16,128]{2,1,0:T(8,128)(2,1)S(1)} %collective-permute-done.far, ...), custom_call_target="tpu_custom_call" | custom-call | flops 2147483648 | bytes 2097152 | tf_op jit(solution)/shard_map/pallas_call | solution.py:340
  16.3 8.0 %collective-permute-start.2 = (bf16[1,16,64,128]{3,2,1,0:T(8,128)(2,1)S(1)}, bf16[1,16,64,128]{3,2,1,0:T(8,128)(2,1)S(1)}, u32[]{:S(2)}, u32[]{:S(2)}) collective-permute-start(bf16[1,16,64,128]{3,2,1,0:T(8,128)(2,1)S(1)} %bitcast.12), channel_id=1, source_target_pairs={{1,0},{2,1},{3,2},{4,3},{5,4},{6,5},{7,6},{8,7},{9,8},{10,9},{11,1... | collective-permute-start | bytes 786440 | tf_op jit(solution)/shard_map/ppermute | solution.py:397
  24.3 1.9 %collective-permute-start.1 = (bf16[1,16,64,128]{3,2,1,0:T(8,128)(2,1)S(1)}, bf16[1,16,64,128]{3,2,1,0:T(8,128)(2,1)S(1)}, u32[]{:S(2)}, u32[]{:S(2)}) collective-permute-start(bf16[1,16,64,128]{3,2,1,0:T(8,128)(2,1)S(1)} %bitcast.11), channel_id=1, source_target_pairs={{0,1},{1,2},{2,3},{3,4},{4,5},{5,6},{6,7},{7,8},{8,9},{9,10},{10,1... | collective-permute-start | bytes 786440 | tf_op jit(solution)/shard_map/ppermute | solution.py:398
  26.3 3.9 %collective-permute-done.2.second = bf16[1,16,64,128]{3,2,1,0:T(8,128)(2,1)S(1)} collective-permute-done((bf16[1,16,64,128]{3,2,1,0:T(8,128)(2,1)S(1)}, bf16[1,16,64,128]{3,2,1,0:T(8,128)(2,1)S(1)}, u32[]{:S(2)}, u32[]{:S(2)}) %collective-permute-start.2) | collective-permute-done | bytes 262176 | tf_op jit(solution)/shard_map/ppermute | solution.py:397
  30.2 4.1 %collective-permute-done.1.first = bf16[1,16,64,128]{3,2,1,0:T(8,128)(2,1)S(1)} collective-permute-done((bf16[1,16,64,128]{3,2,1,0:T(8,128)(2,1)S(1)}, bf16[1,16,64,128]{3,2,1,0:T(8,128)(2,1)S(1)}, u32[]{:S(2)}, u32[]{:S(2)}) %collective-permute-start.1) | collective-permute-done | bytes 262176 | tf_op jit(solution)/shard_map/ppermute | solution.py:398
  34.3 0.8 %shard_map.81 = (bf16[1,16,64,128]{3,2,1,0:T(8,128)(2,1)}, bf16[1,16,64,128]{3,2,1,0:T(8,128)(2,1)}) custom-call(bf16[1,16,64,128]{3,2,1,0:T(8,128)(2,1)S(1)} %collective-permute-done.1.first, bf16[1,16,64,128]{3,2,1,0:T(8,128)(2,1)S(1)} %collective-permute-done.2.second), custom_call_target="tpu_custom_call" | custom-call | bytes 2097152 | tf_op jit(solution)/shard_map/pallas_call | solution.py:340
Async XLA Ops:
  2.3 8.7 %collective-permute-start = (bf16[127,16,128]{2,1,0:T(8,128)(2,1)S(1)}, bf16[127,16,128]{2,1,0:T(8,128)(2,1)S(1)}, u32[]{:S(2)}, u32[]{:S(2)}) collective-permute-start(bf16[127,16,128]{2,1,0:T(8,128)(2,1)S(1)} %get-tuple-element.20), channel_id=1, source_target_pairs={{12,24},{36,48},{60,72},{84,96},{108,120},{132,144},{156,168},{180... | collective-permute-start | bytes 1560584 | tf_op jit(solution)/shard_map/ppermute | solution.py:347
  16.3 13.9 %collective-permute-start.2 = (bf16[1,16,64,128]{3,2,1,0:T(8,128)(2,1)S(1)}, bf16[1,16,64,128]{3,2,1,0:T(8,128)(2,1)S(1)}, u32[]{:S(2)}, u32[]{:S(2)}) collective-permute-start(bf16[1,16,64,128]{3,2,1,0:T(8,128)(2,1)S(1)} %bitcast.12), channel_id=1, source_target_pairs={{1,0},{2,1},{3,2},{4,3},{5,4},{6,5},{7,6},{8,7},{9,8},{10,9},{11,1... | collective-permute-start | bytes 786440 | tf_op jit(solution)/shard_map/ppermute | solution.py:397
  24.3 10.0 %collective-permute-start.1 = (bf16[1,16,64,128]{3,2,1,0:T(8,128)(2,1)S(1)}, bf16[1,16,64,128]{3,2,1,0:T(8,128)(2,1)S(1)}, u32[]{:S(2)}, u32[]{:S(2)}) collective-permute-start(bf16[1,16,64,128]{3,2,1,0:T(8,128)(2,1)S(1)} %bitcast.11), channel_id=1, source_target_pairs={{0,1},{1,2},{2,3},{3,4},{4,5},{5,6},{6,7},{7,8},{8,9},{9,10},{10,1... | collective-permute-start | bytes 786440 | tf_op jit(solution)/shard_map/ppermute | solution.py:398
